TPU v7x, 32 devices: a whole 2x2x4 slice. The times are simulated.
32 devices in a mesh: wide: 16 (over z, y, core), narrow: 2 (over x).
Axes of the slice: x: 2, y: 2, z: 4, core: 2. Of those that a mesh axis runs over, the one named last changes fastest.
Arguments:
- gradient: bfloat16 [40960, 8192], P(('wide', 'narrow')), may hold values from -81 to 81
- seating: int32 [32], replicated, may hold values from 0 to 31, each once
Outputs:
- rotated: bfloat16 [40960, 8192], P(('wide', 'narrow'))
Inputs may be any that keep to these rules, and one draw needn't show every extreme that they name: `seating`: each of the 32 block numbers is the seat of exactly one block.
All inputs are finite; a program needn't handle non-finite values.
Results may differ from a plain program's by a relative error of at most 0.0075.
Values may be sent and summed in bfloat16 or wider, within the bound.
No kernel may reach another device: no remote copies, remote signals or barrier semaphores. Data moves between devices by JAX's collectives and lax.ppermute only.
A program may use at most 128 MiB of HBM per device.

v0:
```python
import functools

import jax
import jax.numpy as jnp
from jax import lax
from jax.experimental import pallas as pl
from jax.experimental.pallas import tpu as pltpu
from jax.sharding import PartitionSpec as P

ROUNDS = 8
LANES = 128
VMEM_LIMIT = 56 * 1024 * 1024


def advance(seat_of, total_slots):
    pair_count = total_slots // 2
    cycle_pos = jnp.where(seat_of % 2 == 0, seat_of // 2 - 1, total_slots - 2 - (seat_of - 1) // 2)
    next_pos = (cycle_pos + 1) % (total_slots - 1)
    new_slot = jnp.where(
        next_pos < pair_count - 1, 2 * (next_pos + 1), 2 * (total_slots - 2 - next_pos) + 1
    )
    return jnp.where(seat_of == 0, 0, new_slot)


def cyclic_masks(width):
    row = lax.broadcasted_iota(jnp.int32, (width, width), 0)
    col = lax.broadcasted_iota(jnp.int32, (width, width), 1)
    gap = col - row
    above = jnp.where(gap < 0, gap + width, gap) < ROUNDS
    below = jnp.where(gap > 0, width - gap, -gap) < ROUNDS
    return above, below


def fold(block, mask):
    width = block.shape[0]
    kept = jnp.where(mask, block, 0.0)
    return jnp.sum(kept.reshape(width // ROUNDS, ROUNDS, width), axis=0)


def unfolded(folded, mask):
    width = folded.shape[1]
    tiled = jnp.broadcast_to(folded[None], (width // ROUNDS, ROUNDS, width))
    return jnp.where(mask, tiled.reshape(width, width), 0.0)


def gram_diagonals(left, right):
    width = left.shape[1]
    above, below = cyclic_masks(width)
    over_rows = (((0,), (0,)), ((), ()))
    dot = functools.partial(
        lax.dot_general, dimension_numbers=over_rows, preferred_element_type=jnp.float32
    )
    cross = dot(left, right)
    return jnp.concatenate(
        [fold(dot(left, left), above), fold(cross, below), fold(cross, above), fold(dot(right, right), above)],
        axis=0,
    )


def pick(planes, index):
    out = planes[0]
    for place in range(1, len(planes)):
        out = jnp.where(index == place, planes[place], out)
    return out


def roll_lanes(plane, shift):
    width = plane.shape[1]
    shift = shift % width
    return plane if shift == 0 else pltpu.roll(plane, shift, 1)


def blend(c, u, s, v, sign):
    if u is None and v is None:
        return None
    if u is None:
        return s * v if sign > 0 else -(s * v)
    if v is None:
        return c * u
    return c * u + s * v if sign > 0 else c * u - s * v


def rotation_diagonals(load):
    lane = lax.broadcasted_iota(jnp.int32, load(0, 0).shape, 1)
    residue = lane % ROUNDS
    quarters = []
    for q in range(4):
        rows = [load(q, s) for s in range(ROUNDS)]
        if q == 1:
            planes = [pick(rows, (residue + d) % ROUNDS) for d in range(ROUNDS)]
            planes = [roll_lanes(plane, d) for d, plane in enumerate(planes)]
        else:
            planes = [pick(rows, (residue - d) % ROUNDS) for d in range(ROUNDS)]
        quarters.append(planes)
    ll, lr, rl, rr = quarters
    ones = jnp.ones_like(ll[0])
    tl, bl = [ones] + [None] * 7, [None] * 8
    tr, br = [None] * 8, [ones] + [None] * 7
    for r in range(ROUNDS):
        a, c, off = ll[0], rr[0], rl[0]
        spread = c - a
        damping = (a + c) / 16.0 + 1e-06
        rest = 4.0 * off * off + damping * damping
        radius = jnp.sqrt(spread * spread + rest)
        falling = spread < 0.0
        reach = radius + jnp.abs(spread)
        tangent = 2.0 * off * jnp.where(falling, reach, 1.0) / jnp.where(falling, rest, reach)
        cs = 1.0 / jnp.sqrt(1.0 + tangent * tangent)
        sn = tangent * cs
        for rows_l, rows_r in ((tl, tr), (bl, br)):
            for o in range(ROUNDS):
                u, v = rows_l[o], rows_r[o]
                rows_l[o] = blend(cs, u, sn, v, -1)
                rows_r[o] = blend(cs, v, sn, u, 1)
        if r + 1 == ROUNDS:
            break
        needed = ROUNDS - r
        new = [[], [], [], []]
        for d in range(needed):
            cl, sl = roll_lanes(cs, d), roll_lanes(sn, d)
            ll1 = cl * ll[d] - sl * lr[d]
            lr1 = sl * ll[d] + cl * lr[d]
            rl1 = cl * rl[d] - sl * rr[d]
            rr1 = sl * rl[d] + cl * rr[d]
            new[0].append(cs * ll1 - sn * rl1)
            new[1].append(cs * lr1 - sn * rr1)
            new[2].append(sn * ll1 + cs * rl1)
            new[3].append(sn * lr1 + cs * rr1)
        ll = new[0][: needed - 1]
        rl = [roll_lanes(plane, -1) for plane in new[2][1:needed]]
        lr = [rl[0]] + new[1][: needed - 2]
        rr = [roll_lanes(plane, -1) for plane in new[3][: needed - 1]]
        for rows_r in (tr, br):
            rows_r[:] = [None] + [
                None if plane is None else roll_lanes(plane, -1) for plane in rows_r[:-1]
            ]
    folded = []
    for rows in (tl, bl):
        folded.append([pick(rows, (s - residue) % ROUNDS) for s in range(ROUNDS)])
    for rows in (tr, br):
        turned = [roll_lanes(plane, ROUNDS - 1) for plane in rows[::-1]]
        folded.append([pick(turned, (residue - s) % ROUNDS) for s in range(ROUNDS)])
    return folded


def find_holders(seat_ref, holder_ref):
    for block in range(holder_ref.shape[0]):
        holder_ref[seat_ref[block]] = block


def block_copies(pair, holder_ref, outer_ref, pair_buffer, sems, inward):
    width = pair_buffer.shape[2] // 2
    copies = []
    for half in range(2):
        column = pl.multiple_of(holder_ref[2 * pair + half] * width, width)
        outer = outer_ref.at[:, pl.ds(column, width)]
        inner = pair_buffer.at[pair, :, pl.ds(half * width, width)]
        source, target = (outer, inner) if inward else (inner, outer)
        copies.append(pltpu.make_async_copy(source, target, sems.at[2 * pair + half]))
    return copies


def start_all(pairs, make):
    def body(pair, carry):
        for copy in make(pair):
            copy.start()
        return carry

    lax.fori_loop(0, pairs, body, 0)


def wait_all(pairs, make):
    def body(pair, carry):
        for copy in make(pair):
            copy.wait()
        return carry

    lax.fori_loop(0, pairs, body, 0)


def put_pair(ref, pair, value):
    rows = pl.ds(pl.multiple_of(pair * 4 * ROUNDS, 4 * ROUNDS), 4 * ROUNDS)
    for part in range(ref.shape[0]):
        ref[part, rows, :] = value[:, part * LANES : (part + 1) * LANES]


def get_quarter(ref, pair, q):
    rows = pl.ds(pl.multiple_of((pair * 4 + q) * ROUNDS, ROUNDS), ROUNDS)
    return jnp.concatenate([ref[part, rows, :] for part in range(ref.shape[0])], axis=1)


def gram_kernel(seat_ref, x_ref, diag_ref, held, holder_ref, in_sems):
    pairs, _, both = held.shape
    width = both // 2
    find_holders(seat_ref, holder_ref)
    arrive = lambda pair: block_copies(pair, holder_ref, x_ref, held, in_sems, True)
    start_all(pairs, arrive)

    def body(pair, carry):
        for copy in arrive(pair):
            copy.wait()
        put_pair(diag_ref, pair, gram_diagonals(held[pair, :, :width], held[pair, :, width:]))
        return carry

    lax.fori_loop(0, pairs, body, 0, unroll=2)


def store_rotation(diag_ref, fold_ref):
    parts, rows, _ = diag_ref.shape
    pairs = rows // (4 * ROUNDS)
    plane = lambda q, s: pl.ds(q * ROUNDS + s, pairs, stride=4 * ROUNDS)
    load = lambda q, s: jnp.concatenate(
        [diag_ref[part, plane(q, s), :] for part in range(parts)], axis=1
    )
    folded = rotation_diagonals(load)
    for q in range(4):
        for s in range(ROUNDS):
            for part in range(parts):
                columns = slice(part * LANES, (part + 1) * LANES)
                fold_ref[part, plane(q, s), :] = folded[q][s][:, columns]


def rotate_pair(pair, held, fold_ref, dense_ref):
    width = held.shape[2] // 2
    above, below = cyclic_masks(width)
    quarter = lambda q: get_quarter(fold_ref, pair, q)
    dense_ref[:width, :width] = unfolded(quarter(0), below).astype(jnp.bfloat16)
    dense_ref[width:, :width] = unfolded(quarter(1), below).astype(jnp.bfloat16)
    dense_ref[:width, width:] = unfolded(quarter(2), above).astype(jnp.bfloat16)
    dense_ref[width:, width:] = unfolded(quarter(3), above).astype(jnp.bfloat16)
    return jnp.dot(held[pair], dense_ref[...], preferred_element_type=jnp.float32)


def apply_kernel(with_gram, seat_ref, diag_ref, x_ref, *refs):
    if with_gram:
        out_ref, next_ref, held, fold_ref, dense_ref, holder_ref, in_sems, out_sems = refs
    else:
        out_ref, held, fold_ref, dense_ref, holder_ref, in_sems, out_sems = refs
    pairs, _, both = held.shape
    width = both // 2
    find_holders(seat_ref, holder_ref)
    arrive = lambda pair: block_copies(pair, holder_ref, x_ref, held, in_sems, True)
    leave = lambda pair: block_copies(pair, holder_ref, out_ref, held, out_sems, False)
    start_all(pairs, arrive)
    store_rotation(diag_ref, fold_ref)

    def next_gram(pair):
        left_seat = jnp.where(pair == 0, 0, jnp.where(pair == 1, 1, 2 * pair - 2))
        right_seat = jnp.where(pair == pairs - 1, 2 * pairs - 2, 2 * pair + 3)

        def block(seat):
            column = pl.multiple_of((seat % 2) * width, width)
            return held[seat // 2, :, pl.ds(column, width)]

        put_pair(next_ref, pair, gram_diagonals(block(left_seat), block(right_seat)))

    def body(step, carry):
        duo = (2 * step, 2 * step + 1)
        for pair in duo:
            for copy in arrive(pair):
                copy.wait()
        turned = [
            rotate_pair(pair, held, fold_ref, dense_ref.at[slot]) for slot, pair in enumerate(duo)
        ]
        for pair, value in zip(duo, turned):
            held[pair] = value.astype(jnp.bfloat16)
        for pair in duo:
            for copy in leave(pair):
                copy.start()
        if with_gram:
            pl.when(step > 0)(lambda: next_gram(duo[0] - 1))
            next_gram(duo[0])
        return carry

    lax.fori_loop(0, pairs // 2, body, 0)
    if with_gram:
        next_gram(pairs - 1)
    wait_all(pairs, leave)


def exchange_stages(axes):
    wide, narrow = (lax.axis_size(axis) for axis in axes)
    lower = [1 << b for b in range(narrow.bit_length() - 1)]
    upper = [narrow << b for b in range(wide.bit_length() - 1)]
    rest = lower + upper[1:]
    return [upper[:1]] + [rest[at : at + 2] for at in range(0, len(rest), 2)]


def sum_over_devices(values, axes):
    count = lax.axis_size(axes)
    index = lax.axis_index(axes)
    held = values.reshape(values.shape[0] * values.shape[1], LANES)

    def spread(choice, bits):
        return sum(bit for place, bit in enumerate(bits) if choice >> place & 1)

    def swap(x, flip):
        return lax.ppermute(x, axes, [(i, i ^ flip) for i in range(count)])

    def place_of(bits):
        return sum(((index & bit) != 0).astype(jnp.int32) << place for place, bit in enumerate(bits))

    stages = exchange_stages(axes)
    for bits in stages:
        group = 1 << len(bits)
        size = held.shape[0] // group
        me = place_of(bits)
        part = lambda place: lax.dynamic_slice_in_dim(held, place * size, size, 0)
        arrived = [swap(part(me ^ other), spread(other, bits)) for other in range(1, group)]
        held = functools.reduce(jnp.add, arrived, part(me))
    for bits in stages[::-1]:
        group = 1 << len(bits)
        me = place_of(bits)
        parts = [held] + [swap(held, spread(other, bits)) for other in range(1, group)]
        for place, _ in enumerate(bits):
            odd = (me >> place & 1) != 0
            step = 1 << place
            parts = [jnp.where(odd, parts[at ^ step], parts[at]) for at in range(group)]
        held = jnp.concatenate(parts, axis=0)
    return held.reshape(values.shape)


def per_device(gradient, seating):
    rows, columns = gradient.shape
    pairs = lax.axis_size("wide")
    width = columns // (2 * pairs)
    everywhere = ("wide", "narrow")
    following = advance(seating, 2 * pairs)

    smem = pl.BlockSpec(memory_space=pltpu.SMEM)
    vmem = pl.BlockSpec(memory_space=pltpu.VMEM)
    hbm = pl.BlockSpec(memory_space=pl.ANY)
    params = pltpu.CompilerParams(vmem_limit_bytes=VMEM_LIMIT)
    held = pltpu.VMEM((pairs, rows, 2 * width), jnp.bfloat16)
    holders = pltpu.SMEM((2 * pairs,), jnp.int32)
    sems = pltpu.SemaphoreType.DMA((2 * pairs,))
    fold = pltpu.VMEM((width // LANES, pairs * 4 * ROUNDS, LANES), jnp.float32)
    dense = pltpu.VMEM((2, 2 * width, 2 * width), jnp.bfloat16)
    diag_shape = jax.ShapeDtypeStruct((width // LANES, pairs * 4 * ROUNDS, LANES), jnp.float32)
    x_shape = jax.ShapeDtypeStruct((rows, columns), jnp.bfloat16)
    gram_flops = 2 * rows * 3 * width * width * pairs
    turn_flops = 2 * rows * 4 * width * width * pairs
    x_bytes = 2 * rows * columns
    cost = lambda flops, moved: pl.CostEstimate(flops=flops, bytes_accessed=moved, transcendentals=0)

    diagonals = pl.pallas_call(
        gram_kernel,
        out_shape=diag_shape,
        in_specs=[smem, hbm],
        out_specs=vmem,
        scratch_shapes=[held, holders, sems],
        compiler_params=params,
        cost_estimate=cost(gram_flops, x_bytes),
        name="gram_of_step_0",
    )(seating, gradient)
    diagonals = sum_over_devices(diagonals, everywhere)

    turned, diagonals = pl.pallas_call(
        functools.partial(apply_kernel, True),
        out_shape=(x_shape, diag_shape),
        in_specs=[smem, vmem, hbm],
        out_specs=(hbm, vmem),
        scratch_shapes=[held, fold, dense, holders, sems, sems],
        compiler_params=params,
        cost_estimate=cost(gram_flops + turn_flops, 2 * x_bytes),
        name="rotate_step_0",
    )(seating, diagonals, gradient)
    diagonals = sum_over_devices(diagonals, everywhere)

    return pl.pallas_call(
        functools.partial(apply_kernel, False),
        out_shape=x_shape,
        in_specs=[smem, vmem, hbm],
        out_specs=hbm,
        scratch_shapes=[held, fold, dense, holders, sems, sems],
        compiler_params=params,
        cost_estimate=cost(turn_flops, 2 * x_bytes),
        name="rotate_step_1",
    )(following, diagonals, turned)


def solution(mesh):
    in_specs = (P(("wide", "narrow"), None), P())
    out_specs = P(("wide", "narrow"), None)
    return jax.shard_map(
        per_device, mesh=mesh, in_specs=in_specs, out_specs=out_specs, check_vma=False
    )
```

profile of v0, /device:TPU:0, one launch (start us, length us, event | category | flops | bytes accessed | tf_op | source)
XLA Modules:
  0.0 139.5 jit_solution(666768258304918374)
XLA Ops:
  0.0 17.1 %gram_of_step_0.1 = f32[2,512,128]{2,1,0:T(8,128)} custom-call(s32[32]{0:T(128)} %seat_ref.3, bf16[1280,8192]{1,0:T(8,128)(2,1)} %x_ref.3), custom_call_target="tpu_custom_call" | custom-call | flops 8053063680 | bytes 20971520 | tf_op jit(solution)/shard_map/gram_of_step_0/pallas_call | solution.py:346
  18.6 1.2 collective-permute-done
  20.8 2.9 %collective-permute-start.1 = (f32[128,128]{1,0:T(8,128)S(1)}, f32[128,128]{1,0:T(8,128)S(1)}, u32[]{:S(2)}, u32[]{:S(2)}) collective-permute-start(f32[128,128]{1,0:T(8,128)S(1)} %get-tuple-element.22), channel_id=1, source_target_pairs={{0,1},{1,0},{2,3},{3,2},{4,5},{5,4},{6,7},{7,6},{8,9},{9,8},{10,11... | collective-permute-start | bytes 196616 | tf_op jit(solution)/shard_map/ppermute | solution.py:298
  23.7 1.6 %collective-permute-start.3 = (f32[128,128]{1,0:T(8,128)S(1)}, f32[128,128]{1,0:T(8,128)S(1)}, u32[]{:S(2)}, u32[]{:S(2)}) collective-permute-start(f32[128,128]{1,0:T(8,128)S(1)} %get-tuple-element.23), channel_id=1, source_target_pairs={{0,5},{1,4},{2,7},{3,6},{4,1},{5,0},{6,3},{7,2},{8,13},{9,12},{10,... | collective-permute-start | bytes 196616 | tf_op jit(solution)/shard_map/ppermute | solution.py:298
  26.1 2.9 %collective-permute-done.3 = f32[128,128]{1,0:T(8,128)S(1)} collective-permute-done((f32[128,128]{1,0:T(8,128)S(1)}, f32[128,128]{1,0:T(8,128)S(1)}, u32[]{:S(2)}, u32[]{:S(2)}) %collective-permute-start.3) | collective-permute-done | bytes 65568 | tf_op jit(solution)/shard_map/ppermute | solution.py:298
  30.1 1.6 %collective-permute-start.4 = (f32[32,128]{1,0:T(8,128)S(1)}, f32[32,128]{1,0:T(8,128)S(1)}, u32[]{:S(2)}, u32[]{:S(2)}) collective-permute-start(f32[32,128]{1,0:T(8,128)S(1)} %get-tuple-element.36), channel_id=1, source_target_pairs={{0,8},{1,9},{2,10},{3,11},{4,12},{5,13},{6,14},{7,15},{8,0},{9,1},... | collective-permute-start | bytes 49160 | tf_op jit(solution)/shard_map/ppermute | solution.py:298
  31.7 2.5 %collective-permute-start.6 = (f32[32,128]{1,0:T(8,128)S(1)}, f32[32,128]{1,0:T(8,128)S(1)}, u32[]{:S(2)}, u32[]{:S(2)}) collective-permute-start(f32[32,128]{1,0:T(8,128)S(1)} %get-tuple-element.37), channel_id=1, source_target_pairs={{0,24},{1,25},{2,26},{3,27},{4,28},{5,29},{6,30},{7,31},{8,16},{9,... | collective-permute-start | bytes 49160 | tf_op jit(solution)/shard_map/ppermute | solution.py:298
  34.3 3.1 %collective-permute-done.6 = f32[32,128]{1,0:T(8,128)S(1)} collective-permute-done((f32[32,128]{1,0:T(8,128)S(1)}, f32[32,128]{1,0:T(8,128)S(1)}, u32[]{:S(2)}, u32[]{:S(2)}) %collective-permute-start.6) | collective-permute-done | bytes 16416 | tf_op jit(solution)/shard_map/ppermute | solution.py:298
  37.4 1.4 %collective-permute-done.5 = f32[32,128]{1,0:T(8,128)S(1)} collective-permute-done((f32[32,128]{1,0:T(8,128)S(1)}, f32[32,128]{1,0:T(8,128)S(1)}, u32[]{:S(2)}, u32[]{:S(2)}) %collective-permute-start.5) | collective-permute-done | bytes 16416 | tf_op jit(solution)/shard_map/ppermute | solution.py:298
  39.6 1.2 collective-permute-start.8
  40.8 2.5 %collective-permute-start.7 = (f32[32,128]{1,0:T(8,128)S(1)}, f32[32,128]{1,0:T(8,128)S(1)}, u32[]{:S(2)}, u32[]{:S(2)}) collective-permute-start(f32[32,128]{1,0:T(8,128)S(1)} %add_add_fusion.3), channel_id=1, source_target_pairs={{0,24},{1,25},{2,26},{3,27},{4,28},{5,29},{6,30},{7,31},{8,16},{9,... | collective-permute-start | bytes 49160 | tf_op jit(solution)/shard_map/ppermute | solution.py:298
  44.3 2.1 %collective-permute-done.7 = f32[32,128]{1,0:T(8,128)S(1)} collective-permute-done((f32[32,128]{1,0:T(8,128)S(1)}, f32[32,128]{1,0:T(8,128)S(1)}, u32[]{:S(2)}, u32[]{:S(2)}) %collective-permute-start.7) | collective-permute-done | bytes 16416 | tf_op jit(solution)/shard_map/ppermute | solution.py:298
  46.3 1.3 collective-permute-start.12
  48.5 1.4 %collective-permute-start.10 = (f32[128,128]{1,0:T(8,128)S(1)}, f32[128,128]{1,0:T(8,128)S(1)}, u32[]{:S(2)}, u32[]{:S(2)}) collective-permute-start(f32[128,128]{1,0:T(8,128)S(1)} %pad_maximum_fusion.4), channel_id=1, source_target_pairs={{0,5},{1,4},{2,7},{3,6},{4,1},{5,0},{6,3},{7,2},{8,13},{9,12},{10,... | collective-permute-start | bytes 196616 | tf_op jit(solution)/shard_map/ppermute | solution.py:298
  50.7 1.2 collective-permute-done.11
  51.9 1.7 %collective-permute-done.10 = f32[128,128]{1,0:T(8,128)S(1)} collective-permute-done((f32[128,128]{1,0:T(8,128)S(1)}, f32[128,128]{1,0:T(8,128)S(1)}, u32[]{:S(2)}, u32[]{:S(2)}) %collective-permute-start.10) | collective-permute-done | bytes 65568 | tf_op jit(solution)/shard_map/ppermute | solution.py:298
  53.8 1.5 %collective-permute-done.13 = f32[512,128]{1,0:T(8,128)S(1)} collective-permute-done((f32[512,128]{1,0:T(8,128)S(1)}, f32[512,128]{1,0:T(8,128)S(1)}, u32[]{:S(2)}, u32[]{:S(2)}) %collective-permute-start.13) | collective-permute-done | bytes 262176 | tf_op jit(solution)/shard_map/ppermute | solution.py:298
  56.2 29.6 %rotate_step_0.1 = (bf16[1280,8192]{1,0:T(8,128)(2,1)}, f32[2,512,128]{2,1,0:T(8,128)}) custom-call(s32[32]{0:T(128)} %seat_ref.3, f32[2,512,128]{2,1,0:T(8,128)} %bitcast.9, bf16[1280,8192]{1,0:T(8,128)(2,1)} %x_ref.3), custom_call_target="tpu_custom_call" | custom-call | flops 18790481920 | bytes 41943040 | tf_op jit(solution)/shard_map/rotate_step_0/pallas_call | solution.py:358
  87.0 1.4 %collective-permute-done.14 = f32[512,128]{1,0:T(8,128)S(1)} collective-permute-done((f32[512,128]{1,0:T(8,128)S(1)}, f32[512,128]{1,0:T(8,128)S(1)}, u32[]{:S(2)}, u32[]{:S(2)}) %collective-permute-start.14) | collective-permute-done | bytes 262176 | tf_op jit(solution)/shard_map/ppermute | solution.py:298
  90.1 2.0 %collective-permute-start.17 = (f32[128,128]{1,0:T(8,128)S(1)}, f32[128,128]{1,0:T(8,128)S(1)}, u32[]{:S(2)}, u32[]{:S(2)}) collective-permute-start(f32[128,128]{1,0:T(8,128)S(1)} %get-tuple-element.17), channel_id=1, source_target_pairs={{0,5},{1,4},{2,7},{3,6},{4,1},{5,0},{6,3},{7,2},{8,13},{9,12},{10,... | collective-permute-start | bytes 196616 | tf_op jit(solution)/shard_map/ppermute | solution.py:298
  93.0 1.2 collective-permute-done.15
  94.2 1.6 %collective-permute-done.17 = f32[128,128]{1,0:T(8,128)S(1)} collective-permute-done((f32[128,128]{1,0:T(8,128)S(1)}, f32[128,128]{1,0:T(8,128)S(1)}, u32[]{:S(2)}, u32[]{:S(2)}) %collective-permute-start.17) | collective-permute-done | bytes 65568 | tf_op jit(solution)/shard_map/ppermute | solution.py:298
  96.8 2.8 %collective-permute-start.20 = (f32[32,128]{1,0:T(8,128)S(1)}, f32[32,128]{1,0:T(8,128)S(1)}, u32[]{:S(2)}, u32[]{:S(2)}) collective-permute-start(f32[32,128]{1,0:T(8,128)S(1)} %get-tuple-element.30), channel_id=1, source_target_pairs={{0,24},{1,25},{2,26},{3,27},{4,28},{5,29},{6,30},{7,31},{8,16},{9,... | collective-permute-start | bytes 49160 | tf_op jit(solution)/shard_map/ppermute | solution.py:298
  100.5 1.9 %collective-permute-done.20 = f32[32,128]{1,0:T(8,128)S(1)} collective-permute-done((f32[32,128]{1,0:T(8,128)S(1)}, f32[32,128]{1,0:T(8,128)S(1)}, u32[]{:S(2)}, u32[]{:S(2)}) %collective-permute-start.20) | collective-permute-done | bytes 16416 | tf_op jit(solution)/shard_map/ppermute | solution.py:298
  102.4 1.8 %collective-permute-done.19 = f32[32,128]{1,0:T(8,128)S(1)} collective-permute-done((f32[32,128]{1,0:T(8,128)S(1)}, f32[32,128]{1,0:T(8,128)S(1)}, u32[]{:S(2)}, u32[]{:S(2)}) %collective-permute-start.19) | collective-permute-done | bytes 16416 | tf_op jit(solution)/shard_map/ppermute | solution.py:298
  106.0 2.7 %collective-permute-start.21 = (f32[32,128]{1,0:T(8,128)S(1)}, f32[32,128]{1,0:T(8,128)S(1)}, u32[]{:S(2)}, u32[]{:S(2)}) collective-permute-start(f32[32,128]{1,0:T(8,128)S(1)} %add_add_fusion.2), channel_id=1, source_target_pairs={{0,24},{1,25},{2,26},{3,27},{4,28},{5,29},{6,30},{7,31},{8,16},{9,... | collective-permute-start | bytes 49160 | tf_op jit(solution)/shard_map/ppermute | solution.py:298
  108.7 1.3 collective-permute-done.22
  110.0 1.5 %collective-permute-done.21 = f32[32,128]{1,0:T(8,128)S(1)} collective-permute-done((f32[32,128]{1,0:T(8,128)S(1)}, f32[32,128]{1,0:T(8,128)S(1)}, u32[]{:S(2)}, u32[]{:S(2)}) %collective-permute-start.21) | collective-permute-done | bytes 16416 | tf_op jit(solution)/shard_map/ppermute | solution.py:298
  111.5 1.1 collective-permute-start.26
  113.5 1.6 %collective-permute-start.24 = (f32[128,128]{1,0:T(8,128)S(1)}, f32[128,128]{1,0:T(8,128)S(1)}, u32[]{:S(2)}, u32[]{:S(2)}) collective-permute-start(f32[128,128]{1,0:T(8,128)S(1)} %pad_maximum_fusion.5), channel_id=1, source_target_pairs={{0,5},{1,4},{2,7},{3,6},{4,1},{5,0},{6,3},{7,2},{8,13},{9,12},{10,... | collective-permute-start | bytes 196616 | tf_op jit(solution)/shard_map/ppermute | solution.py:298
  116.9 1.8 %collective-permute-done.24 = f32[128,128]{1,0:T(8,128)S(1)} collective-permute-done((f32[128,128]{1,0:T(8,128)S(1)}, f32[128,128]{1,0:T(8,128)S(1)}, u32[]{:S(2)}, u32[]{:S(2)}) %collective-permute-start.24) | collective-permute-done | bytes 65568 | tf_op jit(solution)/shard_map/ppermute | solution.py:298
  121.3 18.2 %rotate_step_1.1 = bf16[1280,8192]{1,0:T(8,128)(2,1)} custom-call(s32[32]{0:T(128)} %compare_select_fusion.2.seat_ref, f32[2,512,128]{2,1,0:T(8,128)} %bitcast.4, bf16[1280,8192]{1,0:T(8,128)(2,1)} %get-tuple-element.8.x_ref), custom_call_target="tpu_custom_call" | custom-call | flops 10737418240 | bytes 41943040 | tf_op jit(solution)/shard_map/rotate_step_1/pallas_call | solution.py:370
  (56 shorter events, 21.6 us)
Async XLA Ops:
  18.1 1.6 %collective-permute-start = (f32[512,128]{1,0:T(8,128)S(1)}, f32[512,128]{1,0:T(8,128)S(1)}, u32[]{:S(2)}, u32[]{:S(2)}) collective-permute-start(f32[512,128]{1,0:T(8,128)S(1)} %constant_dynamic-slice_fusion.13), channel_id=1, source_target_pairs={{0,2},{1,3},{2,0},{3,1},{4,6},{5,7},{6,4},{7,5},{8,10},{9,11},{10,... | collective-permute-start | bytes 786440 | tf_op jit(solution)/shard_map/ppermute | solution.py:298
  20.8 5.3 %collective-permute-start.1 = (f32[128,128]{1,0:T(8,128)S(1)}, f32[128,128]{1,0:T(8,128)S(1)}, u32[]{:S(2)}, u32[]{:S(2)}) collective-permute-start(f32[128,128]{1,0:T(8,128)S(1)} %get-tuple-element.22), channel_id=1, source_target_pairs={{0,1},{1,0},{2,3},{3,2},{4,5},{5,4},{6,7},{7,6},{8,9},{9,8},{10,11... | collective-permute-start | bytes 196616 | tf_op jit(solution)/shard_map/ppermute | solution.py:298
  23.7 5.3 %collective-permute-start.3 = (f32[128,128]{1,0:T(8,128)S(1)}, f32[128,128]{1,0:T(8,128)S(1)}, u32[]{:S(2)}, u32[]{:S(2)}) collective-permute-start(f32[128,128]{1,0:T(8,128)S(1)} %get-tuple-element.23), channel_id=1, source_target_pairs={{0,5},{1,4},{2,7},{3,6},{4,1},{5,0},{6,3},{7,2},{8,13},{9,12},{10,... | collective-permute-start | bytes 196616 | tf_op jit(solution)/shard_map/ppermute | solution.py:298
  25.2 4.8 %collective-permute-start.2 = (f32[128,128]{1,0:T(8,128)S(1)}, f32[128,128]{1,0:T(8,128)S(1)}, u32[]{:S(2)}, u32[]{:S(2)}) collective-permute-start(f32[128,128]{1,0:T(8,128)S(1)} %get-tuple-element.24), channel_id=1, source_target_pairs={{0,4},{1,5},{2,6},{3,7},{4,0},{5,1},{6,2},{7,3},{8,12},{9,13},{10,... | collective-permute-start | bytes 196616 | tf_op jit(solution)/shard_map/ppermute | solution.py:298
  30.1 4.2 %collective-permute-start.4 = (f32[32,128]{1,0:T(8,128)S(1)}, f32[32,128]{1,0:T(8,128)S(1)}, u32[]{:S(2)}, u32[]{:S(2)}) collective-permute-start(f32[32,128]{1,0:T(8,128)S(1)} %get-tuple-element.36), channel_id=1, source_target_pairs={{0,8},{1,9},{2,10},{3,11},{4,12},{5,13},{6,14},{7,15},{8,0},{9,1},... | collective-permute-start | bytes 49160 | tf_op jit(solution)/shard_map/ppermute | solution.py:298
  31.7 5.7 %collective-permute-start.6 = (f32[32,128]{1,0:T(8,128)S(1)}, f32[32,128]{1,0:T(8,128)S(1)}, u32[]{:S(2)}, u32[]{:S(2)}) collective-permute-start(f32[32,128]{1,0:T(8,128)S(1)} %get-tuple-element.37), channel_id=1, source_target_pairs={{0,24},{1,25},{2,26},{3,27},{4,28},{5,29},{6,30},{7,31},{8,16},{9,... | collective-permute-start | bytes 49160 | tf_op jit(solution)/shard_map/ppermute | solution.py:298
  34.2 4.6 %collective-permute-start.5 = (f32[32,128]{1,0:T(8,128)S(1)}, f32[32,128]{1,0:T(8,128)S(1)}, u32[]{:S(2)}, u32[]{:S(2)}) collective-permute-start(f32[32,128]{1,0:T(8,128)S(1)} %get-tuple-element.38), channel_id=1, source_target_pairs={{0,16},{1,17},{2,18},{3,19},{4,20},{5,21},{6,22},{7,23},{8,24},{9,... | collective-permute-start | bytes 49160 | tf_op jit(solution)/shard_map/ppermute | solution.py:298
  38.8 4.5 %collective-permute-start.9 = (f32[32,128]{1,0:T(8,128)S(1)}, f32[32,128]{1,0:T(8,128)S(1)}, u32[]{:S(2)}, u32[]{:S(2)}) collective-permute-start(f32[32,128]{1,0:T(8,128)S(1)} %add_add_fusion.3), channel_id=1, source_target_pairs={{0,8},{1,9},{2,10},{3,11},{4,12},{5,13},{6,14},{7,15},{8,0},{9,1},... | collective-permute-start | bytes 49160 | tf_op jit(solution)/shard_map/ppermute | solution.py:298
  39.6 4.6 %collective-permute-start.8 = (f32[32,128]{1,0:T(8,128)S(1)}, f32[32,128]{1,0:T(8,128)S(1)}, u32[]{:S(2)}, u32[]{:S(2)}) collective-permute-start(f32[32,128]{1,0:T(8,128)S(1)} %add_add_fusion.3), channel_id=1, source_target_pairs={{0,16},{1,17},{2,18},{3,19},{4,20},{5,21},{6,22},{7,23},{8,24},{9,... | collective-permute-start | bytes 49160 | tf_op jit(solution)/shard_map/ppermute | solution.py:298
  40.8 5.5 %collective-permute-start.7 = (f32[32,128]{1,0:T(8,128)S(1)}, f32[32,128]{1,0:T(8,128)S(1)}, u32[]{:S(2)}, u32[]{:S(2)}) collective-permute-start(f32[32,128]{1,0:T(8,128)S(1)} %add_add_fusion.3), channel_id=1, source_target_pairs={{0,24},{1,25},{2,26},{3,27},{4,28},{5,29},{6,30},{7,31},{8,16},{9,... | collective-permute-start | bytes 49160 | tf_op jit(solution)/shard_map/ppermute | solution.py:298
  46.3 4.3 %collective-permute-start.12 = (f32[128,128]{1,0:T(8,128)S(1)}, f32[128,128]{1,0:T(8,128)S(1)}, u32[]{:S(2)}, u32[]{:S(2)}) collective-permute-start(f32[128,128]{1,0:T(8,128)S(1)} %pad_maximum_fusion.4), channel_id=1, source_target_pairs={{0,1},{1,0},{2,3},{3,2},{4,5},{5,4},{6,7},{7,6},{8,9},{9,8},{10,11... | collective-permute-start | bytes 196616 | tf_op jit(solution)/shard_map/ppermute | solution.py:298
  47.6 4.3 %collective-permute-start.11 = (f32[128,128]{1,0:T(8,128)S(1)}, f32[128,128]{1,0:T(8,128)S(1)}, u32[]{:S(2)}, u32[]{:S(2)}) collective-permute-start(f32[128,128]{1,0:T(8,128)S(1)} %pad_maximum_fusion.4), channel_id=1, source_target_pairs={{0,4},{1,5},{2,6},{3,7},{4,0},{5,1},{6,2},{7,3},{8,12},{9,13},{10,... | collective-permute-start | bytes 196616 | tf_op jit(solution)/shard_map/ppermute | solution.py:298
  48.5 5.2 %collective-permute-start.10 = (f32[128,128]{1,0:T(8,128)S(1)}, f32[128,128]{1,0:T(8,128)S(1)}, u32[]{:S(2)}, u32[]{:S(2)}) collective-permute-start(f32[128,128]{1,0:T(8,128)S(1)} %pad_maximum_fusion.4), channel_id=1, source_target_pairs={{0,5},{1,4},{2,7},{3,6},{4,1},{5,0},{6,3},{7,2},{8,13},{9,12},{10,... | collective-permute-start | bytes 196616 | tf_op jit(solution)/shard_map/ppermute | solution.py:298
  53.7 1.6 %collective-permute-start.13 = (f32[512,128]{1,0:T(8,128)S(1)}, f32[512,128]{1,0:T(8,128)S(1)}, u32[]{:S(2)}, u32[]{:S(2)}) collective-permute-start(f32[512,128]{1,0:T(8,128)S(1)} %pad_maximum_fusion.2), channel_id=1, source_target_pairs={{0,2},{1,3},{2,0},{3,1},{4,6},{5,7},{6,4},{7,5},{8,10},{9,11},{10,... | collective-permute-start | bytes 786440 | tf_op jit(solution)/shard_map/ppermute | solution.py:298
  56.2 62.7 %copy-start = (s32[32]{0:T(128)S(1)}, s32[32]{0:T(128)}, u32[]{:S(2)}) copy-start(s32[32]{0:T(128)} %seat_ref.3) | copy-start | bytes 388
  86.8 1.6 %collective-permute-start.14 = (f32[512,128]{1,0:T(8,128)S(1)}, f32[512,128]{1,0:T(8,128)S(1)}, u32[]{:S(2)}, u32[]{:S(2)}) collective-permute-start(f32[512,128]{1,0:T(8,128)S(1)} %constant_dynamic-slice_fusion.6), channel_id=1, source_target_pairs={{0,2},{1,3},{2,0},{3,1},{4,6},{5,7},{6,4},{7,5},{8,10},{9,11},{10,... | collective-permute-start | bytes 786440 | tf_op jit(solution)/shard_map/ppermute | solution.py:298
  89.4 4.7 %collective-permute-start.15 = (f32[128,128]{1,0:T(8,128)S(1)}, f32[128,128]{1,0:T(8,128)S(1)}, u32[]{:S(2)}, u32[]{:S(2)}) collective-permute-start(f32[128,128]{1,0:T(8,128)S(1)} %get-tuple-element.16), channel_id=1, source_target_pairs={{0,1},{1,0},{2,3},{3,2},{4,5},{5,4},{6,7},{7,6},{8,9},{9,8},{10,11... | collective-permute-start | bytes 196616 | tf_op jit(solution)/shard_map/ppermute | solution.py:298
  90.1 5.6 %collective-permute-start.17 = (f32[128,128]{1,0:T(8,128)S(1)}, f32[128,128]{1,0:T(8,128)S(1)}, u32[]{:S(2)}, u32[]{:S(2)}) collective-permute-start(f32[128,128]{1,0:T(8,128)S(1)} %get-tuple-element.17), channel_id=1, source_target_pairs={{0,5},{1,4},{2,7},{3,6},{4,1},{5,0},{6,3},{7,2},{8,13},{9,12},{10,... | collective-permute-start | bytes 196616 | tf_op jit(solution)/shard_map/ppermute | solution.py:298
  92.1 4.5 %collective-permute-start.16 = (f32[128,128]{1,0:T(8,128)S(1)}, f32[128,128]{1,0:T(8,128)S(1)}, u32[]{:S(2)}, u32[]{:S(2)}) collective-permute-start(f32[128,128]{1,0:T(8,128)S(1)} %get-tuple-element.18), channel_id=1, source_target_pairs={{0,4},{1,5},{2,6},{3,7},{4,0},{5,1},{6,2},{7,3},{8,12},{9,13},{10,... | collective-permute-start | bytes 196616 | tf_op jit(solution)/shard_map/ppermute | solution.py:298
  96.7 3.8 %collective-permute-start.18 = (f32[32,128]{1,0:T(8,128)S(1)}, f32[32,128]{1,0:T(8,128)S(1)}, u32[]{:S(2)}, u32[]{:S(2)}) collective-permute-start(f32[32,128]{1,0:T(8,128)S(1)} %get-tuple-element.29), channel_id=1, source_target_pairs={{0,8},{1,9},{2,10},{3,11},{4,12},{5,13},{6,14},{7,15},{8,0},{9,1},... | collective-permute-start | bytes 49160 | tf_op jit(solution)/shard_map/ppermute | solution.py:298
  96.8 5.6 %collective-permute-start.20 = (f32[32,128]{1,0:T(8,128)S(1)}, f32[32,128]{1,0:T(8,128)S(1)}, u32[]{:S(2)}, u32[]{:S(2)}) collective-permute-start(f32[32,128]{1,0:T(8,128)S(1)} %get-tuple-element.30), channel_id=1, source_target_pairs={{0,24},{1,25},{2,26},{3,27},{4,28},{5,29},{6,30},{7,31},{8,16},{9,... | collective-permute-start | bytes 49160 | tf_op jit(solution)/shard_map/ppermute | solution.py:298
  99.6 4.6 %collective-permute-start.19 = (f32[32,128]{1,0:T(8,128)S(1)}, f32[32,128]{1,0:T(8,128)S(1)}, u32[]{:S(2)}, u32[]{:S(2)}) collective-permute-start(f32[32,128]{1,0:T(8,128)S(1)} %get-tuple-element.31), channel_id=1, source_target_pairs={{0,16},{1,17},{2,18},{3,19},{4,20},{5,21},{6,22},{7,23},{8,24},{9,... | collective-permute-start | bytes 49160 | tf_op jit(solution)/shard_map/ppermute | solution.py:298
  104.2 4.5 %collective-permute-start.23 = (f32[32,128]{1,0:T(8,128)S(1)}, f32[32,128]{1,0:T(8,128)S(1)}, u32[]{:S(2)}, u32[]{:S(2)}) collective-permute-start(f32[32,128]{1,0:T(8,128)S(1)} %add_add_fusion.2), channel_id=1, source_target_pairs={{0,8},{1,9},{2,10},{3,11},{4,12},{5,13},{6,14},{7,15},{8,0},{9,1},... | collective-permute-start | bytes 49160 | tf_op jit(solution)/shard_map/ppermute | solution.py:298
  105.3 4.6 %collective-permute-start.22 = (f32[32,128]{1,0:T(8,128)S(1)}, f32[32,128]{1,0:T(8,128)S(1)}, u32[]{:S(2)}, u32[]{:S(2)}) collective-permute-start(f32[32,128]{1,0:T(8,128)S(1)} %add_add_fusion.2), channel_id=1, source_target_pairs={{0,16},{1,17},{2,18},{3,19},{4,20},{5,21},{6,22},{7,23},{8,24},{9,... | collective-permute-start | bytes 49160 | tf_op jit(solution)/shard_map/ppermute | solution.py:298
  106.0 5.5 %collective-permute-start.21 = (f32[32,128]{1,0:T(8,128)S(1)}, f32[32,128]{1,0:T(8,128)S(1)}, u32[]{:S(2)}, u32[]{:S(2)}) collective-permute-start(f32[32,128]{1,0:T(8,128)S(1)} %add_add_fusion.2), channel_id=1, source_target_pairs={{0,24},{1,25},{2,26},{3,27},{4,28},{5,29},{6,30},{7,31},{8,16},{9,... | collective-permute-start | bytes 49160 | tf_op jit(solution)/shard_map/ppermute | solution.py:298
  111.5 4.3 %collective-permute-start.26 = (f32[128,128]{1,0:T(8,128)S(1)}, f32[128,128]{1,0:T(8,128)S(1)}, u32[]{:S(2)}, u32[]{:S(2)}) collective-permute-start(f32[128,128]{1,0:T(8,128)S(1)} %pad_maximum_fusion.5), channel_id=1, source_target_pairs={{0,1},{1,0},{2,3},{3,2},{4,5},{5,4},{6,7},{7,6},{8,9},{9,8},{10,11... | collective-permute-start | bytes 196616 | tf_op jit(solution)/shard_map/ppermute | solution.py:298
  112.7 4.3 %collective-permute-start.25 = (f32[128,128]{1,0:T(8,128)S(1)}, f32[128,128]{1,0:T(8,128)S(1)}, u32[]{:S(2)}, u32[]{:S(2)}) collective-permute-start(f32[128,128]{1,0:T(8,128)S(1)} %pad_maximum_fusion.5), channel_id=1, source_target_pairs={{0,4},{1,5},{2,6},{3,7},{4,0},{5,1},{6,2},{7,3},{8,12},{9,13},{10,... | collective-permute-start | bytes 196616 | tf_op jit(solution)/shard_map/ppermute | solution.py:298
  113.5 5.2 %collective-permute-start.24 = (f32[128,128]{1,0:T(8,128)S(1)}, f32[128,128]{1,0:T(8,128)S(1)}, u32[]{:S(2)}, u32[]{:S(2)}) collective-permute-start(f32[128,128]{1,0:T(8,128)S(1)} %pad_maximum_fusion.5), channel_id=1, source_target_pairs={{0,5},{1,4},{2,7},{3,6},{4,1},{5,0},{6,3},{7,2},{8,13},{9,12},{10,... | collective-permute-start | bytes 196616 | tf_op jit(solution)/shard_map/ppermute | solution.py:298
  118.8 1.6 %collective-permute-start.27 = (f32[512,128]{1,0:T(8,128)S(1)}, f32[512,128]{1,0:T(8,128)S(1)}, u32[]{:S(2)}, u32[]{:S(2)}) collective-permute-start(f32[512,128]{1,0:T(8,128)S(1)} %pad_maximum_fusion.3), channel_id=1, source_target_pairs={{0,2},{1,3},{2,0},{3,1},{4,6},{5,7},{6,4},{7,5},{8,10},{9,11},{10,... | collective-permute-start | bytes 786440 | tf_op jit(solution)/shard_map/ppermute | solution.py:298
where the time goes:
time: 140 us
  Pallas kernels  65 us (46%)
  waiting for transfers between devices  35.1 us (25%)
  starting transfers between devices  32.7 us (23%)
  other arithmetic  4.52 us (3%)
  local copies, waits for them, and re-layouts  2.03 us (1%)
    ppermute x28, waiting for transfers between devices, swap(): return lax.ppermute(x, axes, [(i, i ^ flip) for i in range(count)])  35.1 us
    ppermute x28, starting transfers between devices, swap(): return lax.ppermute(x, axes, [(i, i ^ flip) for i in range(count)])  32.7 us
    pallas_call x1, Pallas kernels, per_device(): pl.pallas_call(functools.partial(apply_kernel, True), out_shape=(x_shape,...  29.6 us
    pallas_call x1, Pallas kernels, per_device(): pl.pallas_call(functools.partial(apply_kernel, False), out_shape=x_shape,...  18.2 us
    pallas_call x1, Pallas kernels, per_device(): pl.pallas_call(gram_kernel, out_shape=diag_shape, in_specs=[smem, hbm], o...  17.1 us
  transfers between devices with their start and end apart: 28, of which 25 were waited for; matrix products, arithmetic and copies ran while one was open for 0% of the time, Pallas kernels for 0%

commit v1 on v0

--- a/solution.py
+++ b/solution.py
@@ -50,9 +50,15 @@
     dot = functools.partial(
         lax.dot_general, dimension_numbers=over_rows, preferred_element_type=jnp.float32
     )
-    cross = dot(left, right)
+    wide = dot(left, jnp.concatenate([left, right], axis=1))
+    cross = wide[:, width:]
     return jnp.concatenate(
-        [fold(dot(left, left), above), fold(cross, below), fold(cross, above), fold(dot(right, right), above)],
+        [
+            fold(wide[:, :width], above),
+            fold(cross, below),
+            fold(cross, above),
+            fold(dot(right, right), above),
+        ],
         axis=0,
     )
 
@@ -202,7 +208,7 @@
         put_pair(diag_ref, pair, gram_diagonals(held[pair, :, :width], held[pair, :, width:]))
         return carry
 
-    lax.fori_loop(0, pairs, body, 0, unroll=2)
+    lax.fori_loop(0, pairs, body, 0)
 
 
 def store_rotation(diag_ref, fold_ref):
@@ -278,46 +284,50 @@
     wait_all(pairs, leave)
 
 
-def exchange_stages(axes):
+def sum_over_devices(values, axes, hand_back):
     wide, narrow = (lax.axis_size(axis) for axis in axes)
-    lower = [1 << b for b in range(narrow.bit_length() - 1)]
-    upper = [narrow << b for b in range(wide.bit_length() - 1)]
-    rest = lower + upper[1:]
-    return [upper[:1]] + [rest[at : at + 2] for at in range(0, len(rest), 2)]
-
-
-def sum_over_devices(values, axes):
-    count = lax.axis_size(axes)
+    count = wide * narrow
     index = lax.axis_index(axes)
-    held = values.reshape(values.shape[0] * values.shape[1], LANES)
-
-    def spread(choice, bits):
-        return sum(bit for place, bit in enumerate(bits) if choice >> place & 1)
+    core = narrow
+    chips = [[i for i in range(count) if i & core == kind] for kind in (0, core)]
 
     def swap(x, flip):
         return lax.ppermute(x, axes, [(i, i ^ flip) for i in range(count)])
 
-    def place_of(bits):
-        return sum(((index & bit) != 0).astype(jnp.int32) << place for place, bit in enumerate(bits))
-
-    stages = exchange_stages(axes)
-    for bits in stages:
-        group = 1 << len(bits)
-        size = held.shape[0] // group
-        me = place_of(bits)
-        part = lambda place: lax.dynamic_slice_in_dim(held, place * size, size, 0)
-        arrived = [swap(part(me ^ other), spread(other, bits)) for other in range(1, group)]
-        held = functools.reduce(jnp.add, arrived, part(me))
-    for bits in stages[::-1]:
-        group = 1 << len(bits)
-        me = place_of(bits)
-        parts = [held] + [swap(held, spread(other, bits)) for other in range(1, group)]
-        for place, _ in enumerate(bits):
-            odd = (me >> place & 1) != 0
-            step = 1 << place
-            parts = [jnp.where(odd, parts[at ^ step], parts[at]) for at in range(group)]
-        held = jnp.concatenate(parts, axis=0)
-    return held.reshape(values.shape)
+    def among_chips(x):
+        return lax.all_to_all(
+            x, axes, split_axis=0, concat_axis=0, axis_index_groups=chips, tiled=True
+        )
+
+    held = values.reshape(values.shape[0] * values.shape[1], LANES)
+    half = held.shape[0] // 2
+    odd = (index & core) != 0
+    mine = jnp.where(odd, half, 0)
+    keep = lax.dynamic_slice_in_dim(held, mine, half, 0)
+    send = lax.dynamic_slice_in_dim(held, half - mine, half, 0)
+    held = keep + swap(send, core)
+    size = half // (count // 2)
+    held = jnp.sum(among_chips(held).reshape(count // 2, size, LANES), axis=0)
+    if hand_back == "all_to_all":
+        copies = jnp.broadcast_to(held[None], (count // 2, size, LANES))
+        held = among_chips(copies.reshape(half, LANES))
+    else:
+        bits = [1 << b for b in range(count.bit_length() - 1) if 1 << b != core]
+        for at in range(0, len(bits), 2):
+            pair = bits[at : at + 2]
+            group = 1 << len(pair)
+            flips = [sum(b for p, b in enumerate(pair) if other >> p & 1) for other in range(group)]
+            parts = [held] + [swap(held, flip) for flip in flips[1:]]
+            for place, bit in enumerate(pair):
+                step = 1 << place
+                parts = [
+                    jnp.where((index & bit) != 0, parts[at ^ step], parts[at])
+                    for at in range(group)
+                ]
+            held = jnp.concatenate(parts, axis=0)
+    other = swap(held, core)
+    halves = [jnp.where(odd, other, held), jnp.where(odd, held, other)]
+    return jnp.concatenate(halves, axis=0).reshape(values.shape)
 
 
 def per_device(gradient, seating):
@@ -353,7 +363,7 @@
         cost_estimate=cost(gram_flops, x_bytes),
         name="gram_of_step_0",
     )(seating, gradient)
-    diagonals = sum_over_devices(diagonals, everywhere)
+    diagonals = sum_over_devices(diagonals, everywhere, "all_to_all")
 
     turned, diagonals = pl.pallas_call(
         functools.partial(apply_kernel, True),
@@ -365,7 +375,7 @@
         cost_estimate=cost(gram_flops + turn_flops, 2 * x_bytes),
         name="rotate_step_0",
     )(seating, diagonals, gradient)
-    diagonals = sum_over_devices(diagonals, everywhere)
+    diagonals = sum_over_devices(diagonals, everywhere, "permutes")
 
     return pl.pallas_call(
         functools.partial(apply_kernel, False),

time: 140 us -> 134 us (0.957)
  blocking collectives: 0 us -> 44.5 us
  starting transfers between devices: 32.7 us -> 8.8 us
  waiting for transfers between devices: 35.1 us -> 11.8 us
  Pallas kernels: 65 us -> 62.4 us
    all_to_all x0 -> x3, blocking collectives: none -> 44.5 us  [among_chips(): lax.all_to_all(x, axes, split_axis=0, concat_axis=0, axis_index_groups=ch...]
    ppermute x28 -> x10, starting transfers between devices: 32.7 us -> 8.8 us  [swap(): return lax.ppermute(x, axes, [(i, i ^ flip) for i in range(count)])]
    ppermute x28 -> x10, waiting for transfers between devices: 35.1 us -> 11.8 us  [swap(): return lax.ppermute(x, axes, [(i, i ^ flip) for i in range(count)])]
    pallas_call x1, Pallas kernels: 17.1 us -> 14.7 us  [per_device(): pl.pallas_call(gram_kernel, out_shape=diag_shape, in_specs=[smem, hbm], o...]
    concatenate x6 -> x2, other arithmetic: 1.72 us -> 0.03 us  [sum_over_devices(): held = jnp.concatenate(parts, axis=0)]
    concatenate x0 -> x2, other arithmetic: none -> 1.67 us  [sum_over_devices(): return jnp.concatenate(halves, axis=0).reshape(values.shape)]
  transfers between devices with their start and end apart: 28 -> 10, of which waited for: 25 -> 10; matrix products, arithmetic and copies ran while one was open for 0% -> 0% of each run, Pallas kernels for 0% -> 0%
where the time goes in v1:
time: 134 us
  Pallas kernels  62.4 us (47%)
  blocking collectives  44.5 us (33%)
  waiting for transfers between devices  11.8 us (9%)
  starting transfers between devices  8.8 us (7%)
  other arithmetic  4.35 us (3%)
  local copies, waits for them, and re-layouts  1.97 us (1%)
    all_to_all x3, blocking collectives, among_chips(): lax.all_to_all(x, axes, split_axis=0, concat_axis=0, axis_index_groups=ch...  44.5 us
    pallas_call x1, Pallas kernels, per_device(): pl.pallas_call(functools.partial(apply_kernel, True), out_shape=(x_shape,...  29.5 us
    pallas_call x1, Pallas kernels, per_device(): pl.pallas_call(functools.partial(apply_kernel, False), out_shape=x_shape,...  18.2 us
    pallas_call x1, Pallas kernels, per_device(): pl.pallas_call(gram_kernel, out_shape=diag_shape, in_specs=[smem, hbm], o...  14.7 us
    ppermute x10, waiting for transfers between devices, swap(): return lax.ppermute(x, axes, [(i, i ^ flip) for i in range(count)])  11.8 us
    ppermute x10, starting transfers between devices, swap(): return lax.ppermute(x, axes, [(i, i ^ flip) for i in range(count)])  8.8 us
  transfers between devices with their start and end apart: 10, of which 10 were waited for; matrix products, arithmetic and copies ran while one was open for 0% of the time, Pallas kernels for 0%

profile of v1, /device:TPU:0, one launch (start us, length us, event | category | flops | bytes accessed | tf_op | source)
XLA Modules:
  0.0 134.0 jit_solution(6673181772961203489)
XLA Ops:
  0.0 14.7 %gram_of_step_0.1 = f32[2,512,128]{2,1,0:T(8,128)} custom-call(s32[32]{0:T(128)} %seat_ref.3, bf16[1280,8192]{1,0:T(8,128)(2,1)} %x_ref.3), custom_call_target="tpu_custom_call" | custom-call | flops 8053063680 | bytes 20971520 | tf_op jit(solution)/shard_map/gram_of_step_0/pallas_call | solution.py:356
  14.7 1.0 constant_dynamic-slice_fusion.1
  15.6 0.5 collective-permute-start
  16.2 1.2 collective-permute-done
  17.3 1.0 dynamic-slice_add_fusion.1
  18.3 18.2 %all_to_all.27 = f32[16,32,128]{2,1,0:T(8,128)S(1)} all-to-all(f32[16,32,128]{2,1,0:T(8,128)S(1)} %bitcast.12), channel_id=1, replica_groups={{0,1,4,5,8,9,12,13,16,17,20,21,24,25,28,29},{2,3,6,7,10,11,14,15,18,19,..., dimensions={0} | all-to-all | bytes 524288 | tf_op jit(solution)/shard_map/all_to_all | solution.py:298
  36.6 12.8 %all_to_all.28 = f32[16,32,128]{2,1,0:T(8,128)S(1)} all-to-all(f32[16,32,128]{2,1,0:T(8,128)S(1)} %broadcast_in_dim.4), channel_id=1, replica_groups={{0,1,4,5,8,9,12,13,16,17,20,21,24,25,28,29},{2,3,6,7,10,11,14,15,18,19,..., dimensions={0} | all-to-all | bytes 524288 | tf_op jit(solution)/shard_map/all_to_all | solution.py:298
  49.3 1.5 %collective-permute-done.1 = f32[512,128]{1,0:T(8,128)S(1)} collective-permute-done((f32[512,128]{1,0:T(8,128)S(1)}, f32[512,128]{1,0:T(8,128)S(1)}, u32[]{:S(2)}, u32[]{:S(2)}) %collective-permute-start.1) | collective-permute-done | bytes 262176 | tf_op jit(solution)/shard_map/ppermute | solution.py:295
  50.9 0.8 pad_maximum_fusion
  51.7 29.5 %rotate_step_0.1 = (bf16[1280,8192]{1,0:T(8,128)(2,1)}, f32[2,512,128]{2,1,0:T(8,128)}) custom-call(s32[32]{0:T(128)} %seat_ref.3, f32[2,512,128]{2,1,0:T(8,128)} %bitcast.17, bf16[1280,8192]{1,0:T(8,128)(2,1)} %x_ref.3), custom_call_target="tpu_custom_call" | custom-call | flops 18790481920 | bytes 41943040 | tf_op jit(solution)/shard_map/rotate_step_0/pallas_call | solution.py:368
  81.2 1.0 constant_dynamic-slice_fusion
  82.2 0.2 collective-permute-start.2
  82.4 1.4 %collective-permute-done.2 = f32[512,128]{1,0:T(8,128)S(1)} collective-permute-done((f32[512,128]{1,0:T(8,128)S(1)}, f32[512,128]{1,0:T(8,128)S(1)}, u32[]{:S(2)}, u32[]{:S(2)}) %collective-permute-start.2) | collective-permute-done | bytes 262176 | tf_op jit(solution)/shard_map/ppermute | solution.py:295
  83.8 1.0 dynamic-slice_add_fusion
  84.8 13.5 %all_to_all.29 = f32[16,32,128]{2,1,0:T(8,128)S(1)} all-to-all(f32[16,32,128]{2,1,0:T(8,128)S(1)} %bitcast.11), channel_id=1, replica_groups={{0,1,4,5,8,9,12,13,16,17,20,21,24,25,28,29},{2,3,6,7,10,11,14,15,18,19,..., dimensions={0} | all-to-all | bytes 524288 | tf_op jit(solution)/shard_map/all_to_all | solution.py:298
  98.3 0.8 collective-permute-start.5
  99.2 0.8 collective-permute-start.4
  100.0 1.9 %collective-permute-start.3 = (f32[32,128]{1,0:T(8,128)S(1)}, f32[32,128]{1,0:T(8,128)S(1)}, u32[]{:S(2)}, u32[]{:S(2)}) collective-permute-start(f32[32,128]{1,0:T(8,128)S(1)} %reduce_sum.19), channel_id=1, source_target_pairs={{0,5},{1,4},{2,7},{3,6},{4,1},{5,0},{6,3},{7,2},{8,13},{9,12},{10,... | collective-permute-start | bytes 49160 | tf_op jit(solution)/shard_map/ppermute | solution.py:295
  101.9 0.2 collective-permute-done.5
  102.2 0.8 collective-permute-done.4
  102.9 1.7 %collective-permute-done.3 = f32[32,128]{1,0:T(8,128)S(1)} collective-permute-done((f32[32,128]{1,0:T(8,128)S(1)}, f32[32,128]{1,0:T(8,128)S(1)}, u32[]{:S(2)}, u32[]{:S(2)}) %collective-permute-start.3) | collective-permute-done | bytes 16416 | tf_op jit(solution)/shard_map/ppermute | solution.py:295
  104.7 0.9 collective-permute-start.8
  105.5 1.5 %collective-permute-start.7 = (f32[128,128]{1,0:T(8,128)S(1)}, f32[128,128]{1,0:T(8,128)S(1)}, u32[]{:S(2)}, u32[]{:S(2)}) collective-permute-start(f32[128,128]{1,0:T(8,128)S(1)} %pad_maximum_fusion.3), channel_id=1, source_target_pairs={{0,16},{1,17},{2,18},{3,19},{4,20},{5,21},{6,22},{7,23},{8,24},{9,... | collective-permute-start | bytes 196616 | tf_op jit(solution)/shard_map/ppermute | solution.py:295
  107.0 2.1 %collective-permute-start.6 = (f32[128,128]{1,0:T(8,128)S(1)}, f32[128,128]{1,0:T(8,128)S(1)}, u32[]{:S(2)}, u32[]{:S(2)}) collective-permute-start(f32[128,128]{1,0:T(8,128)S(1)} %pad_maximum_fusion.3), channel_id=1, source_target_pairs={{0,24},{1,25},{2,26},{3,27},{4,28},{5,29},{6,30},{7,31},{8,16},{9,... | collective-permute-start | bytes 196616 | tf_op jit(solution)/shard_map/ppermute | solution.py:295
  109.1 0.3 collective-permute-done.8
  109.4 1.3 collective-permute-done.7
  110.7 2.3 %collective-permute-done.6 = f32[128,128]{1,0:T(8,128)S(1)} collective-permute-done((f32[128,128]{1,0:T(8,128)S(1)}, f32[128,128]{1,0:T(8,128)S(1)}, u32[]{:S(2)}, u32[]{:S(2)}) %collective-permute-start.6) | collective-permute-done | bytes 65568 | tf_op jit(solution)/shard_map/ppermute | solution.py:295
  113.1 0.1 collective-permute-start.9
  113.2 0.5 compare_select_fusion.2.seat_ref
  113.7 1.0 collective-permute-done.9
  114.8 0.8 pad_maximum_fusion.1
  115.6 18.2 %rotate_step_1.1 = bf16[1280,8192]{1,0:T(8,128)(2,1)} custom-call(s32[32]{0:T(128)} %compare_select_fusion.2.seat_ref, f32[2,512,128]{2,1,0:T(8,128)} %bitcast.9, bf16[1280,8192]{1,0:T(8,128)(2,1)} %get-tuple-element.8.x_ref), custom_call_target="tpu_custom_call" | custom-call | flops 10737418240 | bytes 41943040 | tf_op jit(solution)/shard_map/rotate_step_1/pallas_call | solution.py:380
  (13 shorter events, 0.2 us)
Async XLA Ops:
  15.6 1.7 %collective-permute-start = (f32[512,128]{1,0:T(8,128)S(1)}, f32[512,128]{1,0:T(8,128)S(1)}, u32[]{:S(2)}, u32[]{:S(2)}) collective-permute-start(f32[512,128]{1,0:T(8,128)S(1)} %constant_dynamic-slice_fusion.1), channel_id=1, source_target_pairs={{0,2},{1,3},{2,0},{3,1},{4,6},{5,7},{6,4},{7,5},{8,10},{9,11},{10,... | collective-permute-start | bytes 786440 | tf_op jit(solution)/shard_map/ppermute | solution.py:295
  49.3 1.5 %collective-permute-start.1 = (f32[512,128]{1,0:T(8,128)S(1)}, f32[512,128]{1,0:T(8,128)S(1)}, u32[]{:S(2)}, u32[]{:S(2)}) collective-permute-start(f32[512,128]{1,0:T(8,128)S(1)} %bitcast.10), channel_id=1, source_target_pairs={{0,2},{1,3},{2,0},{3,1},{4,6},{5,7},{6,4},{7,5},{8,10},{9,11},{10,... | collective-permute-start | bytes 786440 | tf_op jit(solution)/shard_map/ppermute | solution.py:295
  51.7 61.5 %copy-start = (s32[32]{0:T(128)S(1)}, s32[32]{0:T(128)}, u32[]{:S(2)}) copy-start(s32[32]{0:T(128)} %seat_ref.3) | copy-start | bytes 388
  82.2 1.6 %collective-permute-start.2 = (f32[512,128]{1,0:T(8,128)S(1)}, f32[512,128]{1,0:T(8,128)S(1)}, u32[]{:S(2)}, u32[]{:S(2)}) collective-permute-start(f32[512,128]{1,0:T(8,128)S(1)} %constant_dynamic-slice_fusion), channel_id=1, source_target_pairs={{0,2},{1,3},{2,0},{3,1},{4,6},{5,7},{6,4},{7,5},{8,10},{9,11},{10,... | collective-permute-start | bytes 786440 | tf_op jit(solution)/shard_map/ppermute | solution.py:295
  98.3 3.8 %collective-permute-start.5 = (f32[32,128]{1,0:T(8,128)S(1)}, f32[32,128]{1,0:T(8,128)S(1)}, u32[]{:S(2)}, u32[]{:S(2)}) collective-permute-start(f32[32,128]{1,0:T(8,128)S(1)} %reduce_sum.19), channel_id=1, source_target_pairs={{0,1},{1,0},{2,3},{3,2},{4,5},{5,4},{6,7},{7,6},{8,9},{9,8},{10,11... | collective-permute-start | bytes 49160 | tf_op jit(solution)/shard_map/ppermute | solution.py:295
  99.2 3.7 %collective-permute-start.4 = (f32[32,128]{1,0:T(8,128)S(1)}, f32[32,128]{1,0:T(8,128)S(1)}, u32[]{:S(2)}, u32[]{:S(2)}) collective-permute-start(f32[32,128]{1,0:T(8,128)S(1)} %reduce_sum.19), channel_id=1, source_target_pairs={{0,4},{1,5},{2,6},{3,7},{4,0},{5,1},{6,2},{7,3},{8,12},{9,13},{10,... | collective-permute-start | bytes 49160 | tf_op jit(solution)/shard_map/ppermute | solution.py:295
  100.0 4.6 %collective-permute-start.3 = (f32[32,128]{1,0:T(8,128)S(1)}, f32[32,128]{1,0:T(8,128)S(1)}, u32[]{:S(2)}, u32[]{:S(2)}) collective-permute-start(f32[32,128]{1,0:T(8,128)S(1)} %reduce_sum.19), channel_id=1, source_target_pairs={{0,5},{1,4},{2,7},{3,6},{4,1},{5,0},{6,3},{7,2},{8,13},{9,12},{10,... | collective-permute-start | bytes 49160 | tf_op jit(solution)/shard_map/ppermute | solution.py:295
  104.7 4.7 %collective-permute-start.8 = (f32[128,128]{1,0:T(8,128)S(1)}, f32[128,128]{1,0:T(8,128)S(1)}, u32[]{:S(2)}, u32[]{:S(2)}) collective-permute-start(f32[128,128]{1,0:T(8,128)S(1)} %pad_maximum_fusion.3), channel_id=1, source_target_pairs={{0,8},{1,9},{2,10},{3,11},{4,12},{5,13},{6,14},{7,15},{8,0},{9,1},... | collective-permute-start | bytes 196616 | tf_op jit(solution)/shard_map/ppermute | solution.py:295
  105.5 5.2 %collective-permute-start.7 = (f32[128,128]{1,0:T(8,128)S(1)}, f32[128,128]{1,0:T(8,128)S(1)}, u32[]{:S(2)}, u32[]{:S(2)}) collective-permute-start(f32[128,128]{1,0:T(8,128)S(1)} %pad_maximum_fusion.3), channel_id=1, source_target_pairs={{0,16},{1,17},{2,18},{3,19},{4,20},{5,21},{6,22},{7,23},{8,24},{9,... | collective-permute-start | bytes 196616 | tf_op jit(solution)/shard_map/ppermute | solution.py:295
  107.0 6.1 %collective-permute-start.6 = (f32[128,128]{1,0:T(8,128)S(1)}, f32[128,128]{1,0:T(8,128)S(1)}, u32[]{:S(2)}, u32[]{:S(2)}) collective-permute-start(f32[128,128]{1,0:T(8,128)S(1)} %pad_maximum_fusion.3), channel_id=1, source_target_pairs={{0,24},{1,25},{2,26},{3,27},{4,28},{5,29},{6,30},{7,31},{8,16},{9,... | collective-permute-start | bytes 196616 | tf_op jit(solution)/shard_map/ppermute | solution.py:295
  113.1 1.6 %collective-permute-start.9 = (f32[512,128]{1,0:T(8,128)S(1)}, f32[512,128]{1,0:T(8,128)S(1)}, u32[]{:S(2)}, u32[]{:S(2)}) collective-permute-start(f32[512,128]{1,0:T(8,128)S(1)} %pad_maximum_fusion.2), channel_id=1, source_target_pairs={{0,2},{1,3},{2,0},{3,1},{4,6},{5,7},{6,4},{7,5},{8,10},{9,11},{10,... | collective-permute-start | bytes 786440 | tf_op jit(solution)/shard_map/ppermute | solution.py:295

commit v2 on v1

--- a/solution.py
+++ b/solution.py
@@ -9,7 +9,9 @@
 
 ROUNDS = 8
 LANES = 128
-VMEM_LIMIT = 56 * 1024 * 1024
+STRIP = 16
+AHEAD = 4
+VMEM_LIMIT = 44 * 1024 * 1024
 
 
 def advance(seat_of, total_slots):
@@ -166,7 +168,7 @@
     return copies
 
 
-def start_all(pairs, make):
+def start_each(pairs, make):
     def body(pair, carry):
         for copy in make(pair):
             copy.start()
@@ -184,10 +186,16 @@
     lax.fori_loop(0, pairs, body, 0)
 
 
-def put_pair(ref, pair, value):
+def second_core():
+    return lax.axis_index("wide") % 2 == 1
+
+
+def put_pair(keep_ref, send_ref, pair, value):
     rows = pl.ds(pl.multiple_of(pair * 4 * ROUNDS, 4 * ROUNDS), 4 * ROUNDS)
-    for part in range(ref.shape[0]):
-        ref[part, rows, :] = value[:, part * LANES : (part + 1) * LANES]
+    first, second = value[:, :LANES], value[:, LANES:]
+    odd = second_core()
+    keep_ref[rows, :] = jnp.where(odd, second, first)
+    send_ref[rows, :] = jnp.where(odd, first, second)
 
 
 def get_quarter(ref, pair, q):
@@ -195,29 +203,38 @@
     return jnp.concatenate([ref[part, rows, :] for part in range(ref.shape[0])], axis=1)
 
 
-def gram_kernel(seat_ref, x_ref, diag_ref, held, holder_ref, in_sems):
+def gram_kernel(seat_ref, x_ref, keep_ref, send_ref, held, holder_ref, in_sems):
     pairs, _, both = held.shape
     width = both // 2
     find_holders(seat_ref, holder_ref)
     arrive = lambda pair: block_copies(pair, holder_ref, x_ref, held, in_sems, True)
-    start_all(pairs, arrive)
+    start_each(AHEAD, arrive)
 
     def body(pair, carry):
+        @pl.when(pair + AHEAD < pairs)
+        def _():
+            for copy in arrive(pair + AHEAD):
+                copy.start()
+
         for copy in arrive(pair):
             copy.wait()
-        put_pair(diag_ref, pair, gram_diagonals(held[pair, :, :width], held[pair, :, width:]))
+        put_pair(keep_ref, send_ref, pair, gram_diagonals(held[pair, :, :width], held[pair, :, width:]))
         return carry
 
     lax.fori_loop(0, pairs, body, 0)
 
 
-def store_rotation(diag_ref, fold_ref):
-    parts, rows, _ = diag_ref.shape
+def store_rotation(own_ref, other_ref, fold_ref):
+    parts, rows, _ = fold_ref.shape
     pairs = rows // (4 * ROUNDS)
     plane = lambda q, s: pl.ds(q * ROUNDS + s, pairs, stride=4 * ROUNDS)
-    load = lambda q, s: jnp.concatenate(
-        [diag_ref[part, plane(q, s), :] for part in range(parts)], axis=1
-    )
+    odd = second_core()
+
+    def load(q, s):
+        own, other = own_ref[plane(q, s), :], other_ref[plane(q, s), :]
+        halves = [jnp.where(odd, other, own), jnp.where(odd, own, other)]
+        return jnp.concatenate(halves, axis=1)
+
     folded = rotation_diagonals(load)
     for q in range(4):
         for s in range(ROUNDS):
@@ -230,16 +247,27 @@
     width = held.shape[2] // 2
     above, below = cyclic_masks(width)
     quarter = lambda q: get_quarter(fold_ref, pair, q)
-    dense_ref[:width, :width] = unfolded(quarter(0), below).astype(jnp.bfloat16)
-    dense_ref[width:, :width] = unfolded(quarter(1), below).astype(jnp.bfloat16)
-    dense_ref[:width, width:] = unfolded(quarter(2), above).astype(jnp.bfloat16)
-    dense_ref[width:, width:] = unfolded(quarter(3), above).astype(jnp.bfloat16)
+    for column in range(2):
+        for row in range(2):
+            spread = unfolded(quarter(2 * column + row), above if column else below)
+            spread = spread.astype(jnp.bfloat16)
+            for part in range(0, width, LANES):
+                for other in range(0, width, LANES):
+                    if part == other:
+                        rows = slice(part, part + LANES)
+                    elif column:
+                        rows = slice(part + LANES - STRIP, part + LANES)
+                    else:
+                        rows = slice(part, part + STRIP)
+                    columns = slice(column * width + other, column * width + other + LANES)
+                    shifted = slice(row * width + rows.start, row * width + rows.stop)
+                    dense_ref[shifted, columns] = spread[rows, other : other + LANES]
     return jnp.dot(held[pair], dense_ref[...], preferred_element_type=jnp.float32)
 
 
-def apply_kernel(with_gram, seat_ref, diag_ref, x_ref, *refs):
+def apply_kernel(with_gram, seat_ref, own_ref, other_ref, x_ref, *refs):
     if with_gram:
-        out_ref, next_ref, held, fold_ref, dense_ref, holder_ref, in_sems, out_sems = refs
+        out_ref, keep_ref, send_ref, held, fold_ref, dense_ref, holder_ref, in_sems, out_sems = refs
     else:
         out_ref, held, fold_ref, dense_ref, holder_ref, in_sems, out_sems = refs
     pairs, _, both = held.shape
@@ -247,8 +275,9 @@
     find_holders(seat_ref, holder_ref)
     arrive = lambda pair: block_copies(pair, holder_ref, x_ref, held, in_sems, True)
     leave = lambda pair: block_copies(pair, holder_ref, out_ref, held, out_sems, False)
-    start_all(pairs, arrive)
-    store_rotation(diag_ref, fold_ref)
+    start_each(AHEAD, arrive)
+    dense_ref[...] = jnp.zeros_like(dense_ref)
+    store_rotation(own_ref, other_ref, fold_ref)
 
     def next_gram(pair):
         left_seat = jnp.where(pair == 0, 0, jnp.where(pair == 1, 1, 2 * pair - 2))
@@ -258,10 +287,17 @@
             column = pl.multiple_of((seat % 2) * width, width)
             return held[seat // 2, :, pl.ds(column, width)]
 
-        put_pair(next_ref, pair, gram_diagonals(block(left_seat), block(right_seat)))
+        put_pair(keep_ref, send_ref, pair, gram_diagonals(block(left_seat), block(right_seat)))
 
     def body(step, carry):
         duo = (2 * step, 2 * step + 1)
+
+        @pl.when(2 * step + AHEAD < pairs)
+        def _():
+            for pair in duo:
+                for copy in arrive(pair + AHEAD):
+                    copy.start()
+
         for pair in duo:
             for copy in arrive(pair):
                 copy.wait()
@@ -284,56 +320,31 @@
     wait_all(pairs, leave)
 
 
-def sum_over_devices(values, axes, hand_back):
+def sum_over_devices(keep, send, axes):
     wide, narrow = (lax.axis_size(axis) for axis in axes)
     count = wide * narrow
-    index = lax.axis_index(axes)
-    core = narrow
+    core, group = narrow, count // 2
     chips = [[i for i in range(count) if i & core == kind] for kind in (0, core)]
-
-    def swap(x, flip):
-        return lax.ppermute(x, axes, [(i, i ^ flip) for i in range(count)])
+    partner = [(i, i ^ core) for i in range(count)]
 
     def among_chips(x):
         return lax.all_to_all(
             x, axes, split_axis=0, concat_axis=0, axis_index_groups=chips, tiled=True
         )
 
-    held = values.reshape(values.shape[0] * values.shape[1], LANES)
-    half = held.shape[0] // 2
-    odd = (index & core) != 0
-    mine = jnp.where(odd, half, 0)
-    keep = lax.dynamic_slice_in_dim(held, mine, half, 0)
-    send = lax.dynamic_slice_in_dim(held, half - mine, half, 0)
-    held = keep + swap(send, core)
-    size = half // (count // 2)
-    held = jnp.sum(among_chips(held).reshape(count // 2, size, LANES), axis=0)
-    if hand_back == "all_to_all":
-        copies = jnp.broadcast_to(held[None], (count // 2, size, LANES))
-        held = among_chips(copies.reshape(half, LANES))
-    else:
-        bits = [1 << b for b in range(count.bit_length() - 1) if 1 << b != core]
-        for at in range(0, len(bits), 2):
-            pair = bits[at : at + 2]
-            group = 1 << len(pair)
-            flips = [sum(b for p, b in enumerate(pair) if other >> p & 1) for other in range(group)]
-            parts = [held] + [swap(held, flip) for flip in flips[1:]]
-            for place, bit in enumerate(pair):
-                step = 1 << place
-                parts = [
-                    jnp.where((index & bit) != 0, parts[at ^ step], parts[at])
-                    for at in range(group)
-                ]
-            held = jnp.concatenate(parts, axis=0)
-    other = swap(held, core)
-    halves = [jnp.where(odd, other, held), jnp.where(odd, held, other)]
-    return jnp.concatenate(halves, axis=0).reshape(values.shape)
+    rows = keep.shape[0]
+    held = among_chips(keep + lax.ppermute(send, axes, partner))
+    held = jnp.sum(held.reshape(group, rows // group, LANES), axis=0)
+    copies = jnp.broadcast_to(held[None], (group, rows // group, LANES))
+    own = among_chips(copies.reshape(rows, LANES))
+    return own, lax.ppermute(own, axes, partner)
 
 
 def per_device(gradient, seating):
     rows, columns = gradient.shape
     pairs = lax.axis_size("wide")
     width = columns // (2 * pairs)
+    assert width == 2 * LANES and pairs >= AHEAD
     everywhere = ("wide", "narrow")
     following = advance(seating, 2 * pairs)
 
@@ -346,47 +357,47 @@
     sems = pltpu.SemaphoreType.DMA((2 * pairs,))
     fold = pltpu.VMEM((width // LANES, pairs * 4 * ROUNDS, LANES), jnp.float32)
     dense = pltpu.VMEM((2, 2 * width, 2 * width), jnp.bfloat16)
-    diag_shape = jax.ShapeDtypeStruct((width // LANES, pairs * 4 * ROUNDS, LANES), jnp.float32)
+    diag_shape = jax.ShapeDtypeStruct((pairs * 4 * ROUNDS, LANES), jnp.float32)
     x_shape = jax.ShapeDtypeStruct((rows, columns), jnp.bfloat16)
     gram_flops = 2 * rows * 3 * width * width * pairs
     turn_flops = 2 * rows * 4 * width * width * pairs
     x_bytes = 2 * rows * columns
     cost = lambda flops, moved: pl.CostEstimate(flops=flops, bytes_accessed=moved, transcendentals=0)
 
-    diagonals = pl.pallas_call(
+    keep, send = pl.pallas_call(
         gram_kernel,
-        out_shape=diag_shape,
+        out_shape=(diag_shape, diag_shape),
         in_specs=[smem, hbm],
-        out_specs=vmem,
+        out_specs=(vmem, vmem),
         scratch_shapes=[held, holders, sems],
         compiler_params=params,
         cost_estimate=cost(gram_flops, x_bytes),
         name="gram_of_step_0",
     )(seating, gradient)
-    diagonals = sum_over_devices(diagonals, everywhere, "all_to_all")
-
-    turned, diagonals = pl.pallas_call(
+    own, other = sum_over_devices(keep, send, everywhere)
+
+    turned, keep, send = pl.pallas_call(
         functools.partial(apply_kernel, True),
-        out_shape=(x_shape, diag_shape),
-        in_specs=[smem, vmem, hbm],
-        out_specs=(hbm, vmem),
+        out_shape=(x_shape, diag_shape, diag_shape),
+        in_specs=[smem, vmem, vmem, hbm],
+        out_specs=(hbm, vmem, vmem),
         scratch_shapes=[held, fold, dense, holders, sems, sems],
         compiler_params=params,
         cost_estimate=cost(gram_flops + turn_flops, 2 * x_bytes),
         name="rotate_step_0",
-    )(seating, diagonals, gradient)
-    diagonals = sum_over_devices(diagonals, everywhere, "permutes")
+    )(seating, own, other, gradient)
+    own, other = sum_over_devices(keep, send, everywhere)
 
     return pl.pallas_call(
         functools.partial(apply_kernel, False),
         out_shape=x_shape,
-        in_specs=[smem, vmem, hbm],
+        in_specs=[smem, vmem, vmem, hbm],
         out_specs=hbm,
         scratch_shapes=[held, fold, dense, holders, sems, sems],
         compiler_params=params,
         cost_estimate=cost(turn_flops, 2 * x_bytes),
         name="rotate_step_1",
-    )(following, diagonals, turned)
+    )(following, own, other, turned)
 
 
 def solution(mesh):

time: 134 us -> 127 us (0.948)
  blocking collectives: 44.5 us -> 57.3 us
  starting transfers between devices: 8.8 us -> 0.73 us
  waiting for transfers between devices: 11.8 us -> 5.59 us
  other arithmetic: 4.35 us -> 0.13 us
    all_to_all x3 -> x4, blocking collectives: 44.5 us -> 57.3 us  [among_chips(): lax.all_to_all(x, axes, split_axis=0, concat_axis=0, axis_index_groups=ch...]
    ppermute x10 -> x4, starting transfers between devices: 8.8 us -> 0.73 us  [the longest x2 0.73 us: sum_over_devices(): held = among_chips(keep + lax.ppermute(send, axes, partner))]
    ppermute x10 -> x4, waiting for transfers between devices: 11.8 us -> 5.59 us  [the longest x2 3.04 us: sum_over_devices(): return (own, lax.ppermute(own, axes, partner))]
    dynamic_slice x2 -> x0, local copies, waits for them, and re-layouts: 1.95 us -> none  [sum_over_devices(): send = lax.dynamic_slice_in_dim(held, half - mine, half, 0)]
    add x2, other arithmetic: 1.98 us -> 0.06 us  [sum_over_devices(): held = among_chips(keep + lax.ppermute(send, axes, partner))]
    concatenate x4 -> x0, other arithmetic: 1.7 us -> none  [the longest x2 1.67 us: sum_over_devices(): return jnp.concatenate(halves, axis=0).reshape(values.shape)]
  transfers between devices with their start and end apart: 10 -> 4, of which waited for: 10 -> 4; matrix products, arithmetic and copies ran while one was open for 0% -> 0% of each run, Pallas kernels for 0% -> 0%
where the time goes in v2:
time: 127 us
  Pallas kernels  62.1 us (49%)
  blocking collectives  57.3 us (45%)
  waiting for transfers between devices  5.59 us (4%)
    all_to_all x4, blocking collectives, among_chips(): lax.all_to_all(x, axes, split_axis=0, concat_axis=0, axis_index_groups=ch...  57.3 us
    pallas_call x1, Pallas kernels, per_device(): pl.pallas_call(functools.partial(apply_kernel, True), out_shape=(x_shape,...  29 us
    pallas_call x1, Pallas kernels, per_device(): pl.pallas_call(functools.partial(apply_kernel, False), out_shape=x_shape,...  19.2 us
    pallas_call x1, Pallas kernels, per_device(): pl.pallas_call(gram_kernel, out_shape=(diag_shape, diag_shape), in_specs=...  13.9 us
    ppermute x2, waiting for transfers between devices, sum_over_devices(): return (own, lax.ppermute(own, axes, partner))  3.04 us
    ppermute x2, waiting for transfers between devices, sum_over_devices(): held = among_chips(keep + lax.ppermute(send, axes, partner))  2.55 us
  transfers between devices with their start and end apart: 4, of which 4 were waited for; matrix products, arithmetic and copies ran while one was open for 0% of the time, Pallas kernels for 0%

profile of v2, /device:TPU:0, one launch (start us, length us, event | category | flops | bytes accessed | tf_op | source)
XLA Modules:
  0.0 126.8 jit_solution(9993053637600094014)
XLA Ops:
  0.0 0.0 copy-start
  0.0 0.7 copy-done
  0.7 0.0 copy-start.1
  0.7 13.9 %gram_of_step_0.1 = (f32[512,128]{1,0:T(8,128)S(1)}, f32[512,128]{1,0:T(8,128)S(1)}) custom-call(s32[32]{0:T(128)S(1)} %copy-done, bf16[1280,8192]{1,0:T(8,128)(2,1)} %x_ref.3), custom_call_target="tpu_custom_call" | custom-call | flops 8053063680 | bytes 20971520 | tf_op jit(solution)/shard_map/gram_of_step_0/pallas_call | solution.py:367
  14.5 0.5 collective-permute-start
  15.1 1.2 collective-permute-done
  16.2 18.2 %all_to_all.34 = f32[16,32,128]{2,1,0:T(8,128)S(1)} all-to-all(f32[16,32,128]{2,1,0:T(8,128)S(1)} %bitcast.8), channel_id=1, replica_groups={{0,1,4,5,8,9,12,13,16,17,20,21,24,25,28,29},{2,3,6,7,10,11,14,15,18,19,..., dimensions={0} | all-to-all | bytes 524288 | tf_op jit(solution)/shard_map/all_to_all | solution.py:331
  34.5 12.8 %all_to_all.35 = f32[16,32,128]{2,1,0:T(8,128)S(1)} all-to-all(f32[16,32,128]{2,1,0:T(8,128)S(1)} %broadcast_in_dim.6), channel_id=1, replica_groups={{0,1,4,5,8,9,12,13,16,17,20,21,24,25,28,29},{2,3,6,7,10,11,14,15,18,19,..., dimensions={0} | all-to-all | bytes 524288 | tf_op jit(solution)/shard_map/all_to_all | solution.py:331
  47.3 0.0 collective-permute-start.1
  47.3 1.5 %collective-permute-done.1.other_ref = f32[512,128]{1,0:T(8,128)S(1)} collective-permute-done((f32[512,128]{1,0:T(8,128)S(1)}, f32[512,128]{1,0:T(8,128)S(1)}, u32[]{:S(2)}, u32[]{:S(2)}) %collective-permute-start.1) | collective-permute-done | bytes 262176 | tf_op jit(solution)/shard_map/ppermute | solution.py:340
  48.8 0.0 copy-done.1
  48.8 29.0 %rotate_step_0.1 = (bf16[1280,8192]{1,0:T(8,128)(2,1)}, f32[512,128]{1,0:T(8,128)S(1)}, f32[512,128]{1,0:T(8,128)S(1)}) custom-call(s32[32]{0:T(128)S(1)} %copy-done.1, f32[512,128]{1,0:T(8,128)S(1)} %bitcast.7, f32[512,128]{1,0:T(8,128)S(1)} %collective-permute-done.1.other_ref, bf16[1280,8192]{1,0:T(8,128)(2,1)} %x_ref.3), custom_call_target="tpu_custom_call" | custom-call | flops 18790481920 | bytes 41943040 | tf_op jit(solution)/shard_map/rotate_step_0/pallas_call | solution.py:379
  77.9 0.2 collective-permute-start.2
  78.1 1.4 %collective-permute-done.2 = f32[512,128]{1,0:T(8,128)S(1)} collective-permute-done((f32[512,128]{1,0:T(8,128)S(1)}, f32[512,128]{1,0:T(8,128)S(1)}, u32[]{:S(2)}, u32[]{:S(2)}) %collective-permute-start.2) | collective-permute-done | bytes 262176 | tf_op jit(solution)/shard_map/ppermute | solution.py:336
  79.5 13.5 %all_to_all.36 = f32[16,32,128]{2,1,0:T(8,128)S(1)} all-to-all(f32[16,32,128]{2,1,0:T(8,128)S(1)} %bitcast.9), channel_id=1, replica_groups={{0,1,4,5,8,9,12,13,16,17,20,21,24,25,28,29},{2,3,6,7,10,11,14,15,18,19,..., dimensions={0} | all-to-all | bytes 524288 | tf_op jit(solution)/shard_map/all_to_all | solution.py:331
  93.1 12.8 %all_to_all.37 = f32[16,32,128]{2,1,0:T(8,128)S(1)} all-to-all(f32[16,32,128]{2,1,0:T(8,128)S(1)} %broadcast_in_dim.7), channel_id=1, replica_groups={{0,1,4,5,8,9,12,13,16,17,20,21,24,25,28,29},{2,3,6,7,10,11,14,15,18,19,..., dimensions={0} | all-to-all | bytes 524288 | tf_op jit(solution)/shard_map/all_to_all | solution.py:331
  105.8 0.0 collective-permute-start.3
  105.9 1.5 %collective-permute-done.3.other_ref = f32[512,128]{1,0:T(8,128)S(1)} collective-permute-done((f32[512,128]{1,0:T(8,128)S(1)}, f32[512,128]{1,0:T(8,128)S(1)}, u32[]{:S(2)}, u32[]{:S(2)}) %collective-permute-start.3) | collective-permute-done | bytes 262176 | tf_op jit(solution)/shard_map/ppermute | solution.py:340
  107.4 19.2 %rotate_step_1.1 = bf16[1280,8192]{1,0:T(8,128)(2,1)} custom-call(s32[32]{0:T(128)S(1)} %compare_select_fusion.2.seat_ref, f32[512,128]{1,0:T(8,128)S(1)} %bitcast.5, f32[512,128]{1,0:T(8,128)S(1)} %collective-permute-done.3.other_ref, bf16[1280,8192]{1,0:T(8,128)(2,1)} %get-tuple-element.14.x_ref), custom_call_target="tpu_custom_call" | custom-call | flops 10737418240 | bytes 41943040 | tf_op jit(solution)/shard_map/rotate_step_1/pallas_call | solution.py:391
  (7 shorter events, 0.2 us)
Async XLA Ops:
  0.0 0.7 copy-start
  0.7 48.2 %copy-start.1 = (s32[32]{0:T(128)S(1)}, s32[32]{0:T(128)}, u32[]{:S(2)}) copy-start(s32[32]{0:T(128)} %seat_ref.3) | copy-start | bytes 388
  14.5 1.7 %collective-permute-start = (f32[512,128]{1,0:T(8,128)S(1)}, f32[512,128]{1,0:T(8,128)S(1)}, u32[]{:S(2)}, u32[]{:S(2)}) collective-permute-start(f32[512,128]{1,0:T(8,128)S(1)} %get-tuple-element.11), channel_id=1, source_target_pairs={{0,2},{1,3},{2,0},{3,1},{4,6},{5,7},{6,4},{7,5},{8,10},{9,11},{10,... | collective-permute-start | bytes 786440 | tf_op jit(solution)/shard_map/ppermute | solution.py:336
  47.3 1.5 %collective-permute-start.1 = (f32[512,128]{1,0:T(8,128)S(1)}, f32[512,128]{1,0:T(8,128)S(1)}, u32[]{:S(2)}, u32[]{:S(2)}) collective-permute-start(f32[512,128]{1,0:T(8,128)S(1)} %bitcast.6), channel_id=1, source_target_pairs={{0,2},{1,3},{2,0},{3,1},{4,6},{5,7},{6,4},{7,5},{8,10},{9,11},{10,... | collective-permute-start | bytes 786440 | tf_op jit(solution)/shard_map/ppermute | solution.py:340
  77.9 1.6 %collective-permute-start.2 = (f32[512,128]{1,0:T(8,128)S(1)}, f32[512,128]{1,0:T(8,128)S(1)}, u32[]{:S(2)}, u32[]{:S(2)}) collective-permute-start(f32[512,128]{1,0:T(8,128)S(1)} %get-tuple-element.13), channel_id=1, source_target_pairs={{0,2},{1,3},{2,0},{3,1},{4,6},{5,7},{6,4},{7,5},{8,10},{9,11},{10,... | collective-permute-start | bytes 786440 | tf_op jit(solution)/shard_map/ppermute | solution.py:336
  105.8 1.5 %collective-permute-start.3 = (f32[512,128]{1,0:T(8,128)S(1)}, f32[512,128]{1,0:T(8,128)S(1)}, u32[]{:S(2)}, u32[]{:S(2)}) collective-permute-start(f32[512,128]{1,0:T(8,128)S(1)} %bitcast.4), channel_id=1, source_target_pairs={{0,2},{1,3},{2,0},{3,1},{4,6},{5,7},{6,4},{7,5},{8,10},{9,11},{10,... | collective-permute-start | bytes 786440 | tf_op jit(solution)/shard_map/ppermute | solution.py:340

commit v3 on v2

--- a/solution.py
+++ b/solution.py
@@ -24,30 +24,32 @@
     return jnp.where(seat_of == 0, 0, new_slot)
 
 
-def cyclic_masks(width):
-    row = lax.broadcasted_iota(jnp.int32, (width, width), 0)
-    col = lax.broadcasted_iota(jnp.int32, (width, width), 1)
+def window_masks(rows, before):
+    row = lax.broadcasted_iota(jnp.int32, (rows, LANES), 0) - before
+    col = lax.broadcasted_iota(jnp.int32, (rows, LANES), 1)
     gap = col - row
-    above = jnp.where(gap < 0, gap + width, gap) < ROUNDS
-    below = jnp.where(gap > 0, width - gap, -gap) < ROUNDS
-    return above, below
-
-
-def fold(block, mask):
+    return (gap >= 0) & (gap < ROUNDS), (gap <= 0) & (gap > -ROUNDS)
+
+
+def fold(block, upper):
     width = block.shape[0]
-    kept = jnp.where(mask, block, 0.0)
-    return jnp.sum(kept.reshape(width // ROUNDS, ROUNDS, width), axis=0)
-
-
-def unfolded(folded, mask):
-    width = folded.shape[1]
-    tiled = jnp.broadcast_to(folded[None], (width // ROUNDS, ROUNDS, width))
-    return jnp.where(mask, tiled.reshape(width, width), 0.0)
+    before = ROUNDS if upper else 0
+    window = LANES + ROUNDS
+    mask = window_masks(window, before)[0 if upper else 1]
+    parts = []
+    for part in range(0, width, LANES):
+        strip = (part - ROUNDS if upper else part + LANES) % width
+        pieces = [
+            block[strip : strip + ROUNDS, part : part + LANES],
+            block[part : part + LANES, part : part + LANES],
+        ]
+        kept = jnp.where(mask, jnp.concatenate(pieces if upper else pieces[::-1], axis=0), 0.0)
+        parts.append(jnp.sum(kept.reshape(window // ROUNDS, ROUNDS, LANES), axis=0))
+    return jnp.concatenate(parts, axis=1)
 
 
 def gram_diagonals(left, right):
     width = left.shape[1]
-    above, below = cyclic_masks(width)
     over_rows = (((0,), (0,)), ((), ()))
     dot = functools.partial(
         lax.dot_general, dimension_numbers=over_rows, preferred_element_type=jnp.float32
@@ -56,20 +58,25 @@
     cross = wide[:, width:]
     return jnp.concatenate(
         [
-            fold(wide[:, :width], above),
-            fold(cross, below),
-            fold(cross, above),
-            fold(dot(right, right), above),
+            fold(wide[:, :width], True),
+            fold(cross, False),
+            fold(cross, True),
+            fold(dot(right, right), True),
         ],
         axis=0,
     )
 
 
-def pick(planes, index):
-    out = planes[0]
-    for place in range(1, len(planes)):
-        out = jnp.where(index == place, planes[place], out)
-    return out
+def turn(planes, sign):
+    lane = lax.broadcasted_iota(jnp.int32, planes[0].shape, 1)
+    step = 1
+    while step < ROUNDS:
+        moves = (lane & step) != 0
+        planes = [
+            jnp.where(moves, planes[(j + sign * step) % ROUNDS], planes[j]) for j in range(ROUNDS)
+        ]
+        step *= 2
+    return planes
 
 
 def roll_lanes(plane, shift):
@@ -89,30 +96,26 @@
 
 
 def rotation_diagonals(load):
-    lane = lax.broadcasted_iota(jnp.int32, load(0, 0).shape, 1)
-    residue = lane % ROUNDS
     quarters = []
     for q in range(4):
-        rows = [load(q, s) for s in range(ROUNDS)]
+        turned = turn([load(q, s) for s in range(ROUNDS)], 1)
         if q == 1:
-            planes = [pick(rows, (residue + d) % ROUNDS) for d in range(ROUNDS)]
-            planes = [roll_lanes(plane, d) for d, plane in enumerate(planes)]
+            quarters.append([roll_lanes(turned[d], d) for d in range(ROUNDS)])
         else:
-            planes = [pick(rows, (residue - d) % ROUNDS) for d in range(ROUNDS)]
-        quarters.append(planes)
-    ll, lr, rl, rr = quarters
+            quarters.append([turned[-d] for d in range(ROUNDS)])
+    ll, lr, rl, rr = (dict(enumerate(planes)) for planes in quarters)
+    for d in range(1, ROUNDS):
+        ll[-d], rr[-d] = roll_lanes(ll[d], -d), roll_lanes(rr[d], -d)
+        lr[-d], rl[-d] = roll_lanes(rl[d], -d), roll_lanes(lr[d], -d)
     ones = jnp.ones_like(ll[0])
     tl, bl = [ones] + [None] * 7, [None] * 8
     tr, br = [None] * 8, [ones] + [None] * 7
     for r in range(ROUNDS):
-        a, c, off = ll[0], rr[0], rl[0]
+        a, c, off = ll[0], rr[0], lr[0]
         spread = c - a
         damping = (a + c) / 16.0 + 1e-06
-        rest = 4.0 * off * off + damping * damping
-        radius = jnp.sqrt(spread * spread + rest)
-        falling = spread < 0.0
-        reach = radius + jnp.abs(spread)
-        tangent = 2.0 * off * jnp.where(falling, reach, 1.0) / jnp.where(falling, rest, reach)
+        radius = jnp.sqrt(spread * spread + 4.0 * off * off + damping * damping)
+        tangent = 2.0 * off / (spread + radius)
         cs = 1.0 / jnp.sqrt(1.0 + tangent * tangent)
         sn = tangent * cs
         for rows_l, rows_r in ((tl, tr), (bl, br)):
@@ -122,32 +125,33 @@
                 rows_r[o] = blend(cs, v, sn, u, 1)
         if r + 1 == ROUNDS:
             break
-        needed = ROUNDS - r
-        new = [[], [], [], []]
-        for d in range(needed):
+        reach = ROUNDS - 1 - r
+        new = [{}, {}, {}, {}]
+        for d in range(-reach, reach + 1):
             cl, sl = roll_lanes(cs, d), roll_lanes(sn, d)
             ll1 = cl * ll[d] - sl * lr[d]
             lr1 = sl * ll[d] + cl * lr[d]
             rl1 = cl * rl[d] - sl * rr[d]
             rr1 = sl * rl[d] + cl * rr[d]
-            new[0].append(cs * ll1 - sn * rl1)
-            new[1].append(cs * lr1 - sn * rr1)
-            new[2].append(sn * ll1 + cs * rl1)
-            new[3].append(sn * lr1 + cs * rr1)
-        ll = new[0][: needed - 1]
-        rl = [roll_lanes(plane, -1) for plane in new[2][1:needed]]
-        lr = [rl[0]] + new[1][: needed - 2]
-        rr = [roll_lanes(plane, -1) for plane in new[3][: needed - 1]]
+            new[0][d] = cs * ll1 - sn * rl1
+            new[1][d] = cs * lr1 - sn * rr1
+            new[2][d] = sn * ll1 + cs * rl1
+            new[3][d] = sn * lr1 + cs * rr1
+        inner = range(1 - reach, reach)
+        ll = {d: new[0][d] for d in inner}
+        lr = {d: new[1][d - 1] for d in inner}
+        rl = {d: roll_lanes(new[2][d + 1], -1) for d in inner}
+        rr = {d: roll_lanes(new[3][d], -1) for d in inner}
         for rows_r in (tr, br):
             rows_r[:] = [None] + [
                 None if plane is None else roll_lanes(plane, -1) for plane in rows_r[:-1]
             ]
     folded = []
     for rows in (tl, bl):
-        folded.append([pick(rows, (s - residue) % ROUNDS) for s in range(ROUNDS)])
+        folded.append(turn(rows, -1))
     for rows in (tr, br):
-        turned = [roll_lanes(plane, ROUNDS - 1) for plane in rows[::-1]]
-        folded.append([pick(turned, (residue - s) % ROUNDS) for s in range(ROUNDS)])
+        turned = turn([roll_lanes(plane, ROUNDS - 1) for plane in rows[::-1]], 1)
+        folded.append([turned[-s] for s in range(ROUNDS)])
     return folded
 
 
@@ -245,23 +249,23 @@
 
 def rotate_pair(pair, held, fold_ref, dense_ref):
     width = held.shape[2] // 2
-    above, below = cyclic_masks(width)
-    quarter = lambda q: get_quarter(fold_ref, pair, q)
+    window = LANES + STRIP
+    above = window_masks(window, STRIP)[0]
+    below = window_masks(window, 0)[1]
     for column in range(2):
         for row in range(2):
-            spread = unfolded(quarter(2 * column + row), above if column else below)
-            spread = spread.astype(jnp.bfloat16)
+            folded = get_quarter(fold_ref, pair, 2 * column + row)
             for part in range(0, width, LANES):
-                for other in range(0, width, LANES):
-                    if part == other:
-                        rows = slice(part, part + LANES)
-                    elif column:
-                        rows = slice(part + LANES - STRIP, part + LANES)
-                    else:
-                        rows = slice(part, part + STRIP)
-                    columns = slice(column * width + other, column * width + other + LANES)
-                    shifted = slice(row * width + rows.start, row * width + rows.stop)
-                    dense_ref[shifted, columns] = spread[rows, other : other + LANES]
+                tiled = jnp.broadcast_to(
+                    folded[None, :, part : part + LANES], (window // ROUNDS, ROUNDS, LANES)
+                ).reshape(window, LANES)
+                spread = jnp.where(above if column else below, tiled, 0.0).astype(jnp.bfloat16)
+                block = spread[STRIP:] if column else spread[:LANES]
+                beside = spread[:STRIP] if column else spread[LANES:]
+                strip = row * width + (part - STRIP if column else part + LANES) % width
+                columns = slice(column * width + part, column * width + part + LANES)
+                dense_ref[row * width + part : row * width + part + LANES, columns] = block
+                dense_ref[strip : strip + STRIP, columns] = beside
     return jnp.dot(held[pair], dense_ref[...], preferred_element_type=jnp.float32)
 
 
@@ -275,7 +279,7 @@
     find_holders(seat_ref, holder_ref)
     arrive = lambda pair: block_copies(pair, holder_ref, x_ref, held, in_sems, True)
     leave = lambda pair: block_copies(pair, holder_ref, out_ref, held, out_sems, False)
-    start_each(AHEAD, arrive)
+    start_each(pairs, arrive)
     dense_ref[...] = jnp.zeros_like(dense_ref)
     store_rotation(own_ref, other_ref, fold_ref)
 
@@ -291,12 +295,6 @@
 
     def body(step, carry):
         duo = (2 * step, 2 * step + 1)
-
-        @pl.when(2 * step + AHEAD < pairs)
-        def _():
-            for pair in duo:
-                for copy in arrive(pair + AHEAD):
-                    copy.start()
 
         for pair in duo:
             for copy in arrive(pair):

time: 127 us -> 127 us (level)
  no operation moved by 1% of the time
where the time goes in v3:
time: 127 us; the launch traced here: 126 us
  Pallas kernels  61.7 us (49%)
  blocking collectives  57.3 us (45%)
  waiting for transfers between devices  5.59 us (4%)
    all_to_all x4, blocking collectives, among_chips(): lax.all_to_all(x, axes, split_axis=0, concat_axis=0, axis_index_groups=ch...  57.3 us
    pallas_call x1, Pallas kernels, per_device(): pl.pallas_call(functools.partial(apply_kernel, True), out_shape=(x_shape,...  29.1 us
    pallas_call x1, Pallas kernels, per_device(): pl.pallas_call(functools.partial(apply_kernel, False), out_shape=x_shape,...  18.6 us
    pallas_call x1, Pallas kernels, per_device(): pl.pallas_call(gram_kernel, out_shape=(diag_shape, diag_shape), in_specs=...  14.1 us
    ppermute x2, waiting for transfers between devices, sum_over_devices(): return (own, lax.ppermute(own, axes, partner))  3.04 us
    ppermute x2, waiting for transfers between devices, sum_over_devices(): held = among_chips(keep + lax.ppermute(send, axes, partner))  2.56 us
  transfers between devices with their start and end apart: 4, of which 4 were waited for; matrix products, arithmetic and copies ran while one was open for 0% of the time, Pallas kernels for 0%

profile of v3, /device:TPU:0, one launch (start us, length us, event | category | flops | bytes accessed | tf_op | source)
XLA Modules:
  0.0 126.4 jit_solution(16346093403666771578)
XLA Ops:
  0.0 0.0 copy-start
  0.0 0.7 copy-done
  0.7 0.0 copy-start.1
  0.7 14.1 %gram_of_step_0.1 = (f32[512,128]{1,0:T(8,128)S(1)}, f32[512,128]{1,0:T(8,128)S(1)}) custom-call(s32[32]{0:T(128)S(1)} %copy-done, bf16[1280,8192]{1,0:T(8,128)(2,1)} %x_ref.3), custom_call_target="tpu_custom_call" | custom-call | flops 8053063680 | bytes 20971520 | tf_op jit(solution)/shard_map/gram_of_step_0/pallas_call | solution.py:365
  14.7 0.5 collective-permute-start
  15.3 1.2 collective-permute-done
  16.5 18.2 %all_to_all.34 = f32[16,32,128]{2,1,0:T(8,128)S(1)} all-to-all(f32[16,32,128]{2,1,0:T(8,128)S(1)} %bitcast.8), channel_id=1, replica_groups={{0,1,4,5,8,9,12,13,16,17,20,21,24,25,28,29},{2,3,6,7,10,11,14,15,18,19,..., dimensions={0} | all-to-all | bytes 524288 | tf_op jit(solution)/shard_map/all_to_all | solution.py:329
  34.7 12.8 %all_to_all.35 = f32[16,32,128]{2,1,0:T(8,128)S(1)} all-to-all(f32[16,32,128]{2,1,0:T(8,128)S(1)} %broadcast_in_dim.6), channel_id=1, replica_groups={{0,1,4,5,8,9,12,13,16,17,20,21,24,25,28,29},{2,3,6,7,10,11,14,15,18,19,..., dimensions={0} | all-to-all | bytes 524288 | tf_op jit(solution)/shard_map/all_to_all | solution.py:329
  47.5 0.0 collective-permute-start.1
  47.5 1.5 %collective-permute-done.1.other_ref = f32[512,128]{1,0:T(8,128)S(1)} collective-permute-done((f32[512,128]{1,0:T(8,128)S(1)}, f32[512,128]{1,0:T(8,128)S(1)}, u32[]{:S(2)}, u32[]{:S(2)}) %collective-permute-start.1) | collective-permute-done | bytes 262176 | tf_op jit(solution)/shard_map/ppermute | solution.py:338
  49.0 0.0 copy-done.1
  49.0 29.1 %rotate_step_0.1 = (bf16[1280,8192]{1,0:T(8,128)(2,1)}, f32[512,128]{1,0:T(8,128)S(1)}, f32[512,128]{1,0:T(8,128)S(1)}) custom-call(s32[32]{0:T(128)S(1)} %copy-done.1, f32[512,128]{1,0:T(8,128)S(1)} %bitcast.7, f32[512,128]{1,0:T(8,128)S(1)} %collective-permute-done.1.other_ref, bf16[1280,8192]{1,0:T(8,128)(2,1)} %x_ref.3), custom_call_target="tpu_custom_call" | custom-call | flops 18790481920 | bytes 41943040 | tf_op jit(solution)/shard_map/rotate_step_0/pallas_call | solution.py:377
  78.1 0.2 collective-permute-start.2
  78.3 1.4 %collective-permute-done.2 = f32[512,128]{1,0:T(8,128)S(1)} collective-permute-done((f32[512,128]{1,0:T(8,128)S(1)}, f32[512,128]{1,0:T(8,128)S(1)}, u32[]{:S(2)}, u32[]{:S(2)}) %collective-permute-start.2) | collective-permute-done | bytes 262176 | tf_op jit(solution)/shard_map/ppermute | solution.py:334
  79.7 13.5 %all_to_all.36 = f32[16,32,128]{2,1,0:T(8,128)S(1)} all-to-all(f32[16,32,128]{2,1,0:T(8,128)S(1)} %bitcast.9), channel_id=1, replica_groups={{0,1,4,5,8,9,12,13,16,17,20,21,24,25,28,29},{2,3,6,7,10,11,14,15,18,19,..., dimensions={0} | all-to-all | bytes 524288 | tf_op jit(solution)/shard_map/all_to_all | solution.py:329
  93.3 12.8 %all_to_all.37 = f32[16,32,128]{2,1,0:T(8,128)S(1)} all-to-all(f32[16,32,128]{2,1,0:T(8,128)S(1)} %broadcast_in_dim.7), channel_id=1, replica_groups={{0,1,4,5,8,9,12,13,16,17,20,21,24,25,28,29},{2,3,6,7,10,11,14,15,18,19,..., dimensions={0} | all-to-all | bytes 524288 | tf_op jit(solution)/shard_map/all_to_all | solution.py:329
  106.1 0.0 collective-permute-start.3
  106.1 1.5 %collective-permute-done.3.other_ref = f32[512,128]{1,0:T(8,128)S(1)} collective-permute-done((f32[512,128]{1,0:T(8,128)S(1)}, f32[512,128]{1,0:T(8,128)S(1)}, u32[]{:S(2)}, u32[]{:S(2)}) %collective-permute-start.3) | collective-permute-done | bytes 262176 | tf_op jit(solution)/shard_map/ppermute | solution.py:338
  107.6 18.6 %rotate_step_1.1 = bf16[1280,8192]{1,0:T(8,128)(2,1)} custom-call(s32[32]{0:T(128)S(1)} %compare_select_fusion.2.seat_ref, f32[512,128]{1,0:T(8,128)S(1)} %bitcast.5, f32[512,128]{1,0:T(8,128)S(1)} %collective-permute-done.3.other_ref, bf16[1280,8192]{1,0:T(8,128)(2,1)} %get-tuple-element.14.x_ref), custom_call_target="tpu_custom_call" | custom-call | flops 10737418240 | bytes 41943040 | tf_op jit(solution)/shard_map/rotate_step_1/pallas_call | solution.py:389
  (7 shorter events, 0.2 us)
Async XLA Ops:
  0.0 0.7 copy-start
  0.7 48.4 %copy-start.1 = (s32[32]{0:T(128)S(1)}, s32[32]{0:T(128)}, u32[]{:S(2)}) copy-start(s32[32]{0:T(128)} %seat_ref.3) | copy-start | bytes 388
  14.7 1.7 %collective-permute-start = (f32[512,128]{1,0:T(8,128)S(1)}, f32[512,128]{1,0:T(8,128)S(1)}, u32[]{:S(2)}, u32[]{:S(2)}) collective-permute-start(f32[512,128]{1,0:T(8,128)S(1)} %get-tuple-element.11), channel_id=1, source_target_pairs={{0,2},{1,3},{2,0},{3,1},{4,6},{5,7},{6,4},{7,5},{8,10},{9,11},{10,... | collective-permute-start | bytes 786440 | tf_op jit(solution)/shard_map/ppermute | solution.py:334
  47.5 1.5 %collective-permute-start.1 = (f32[512,128]{1,0:T(8,128)S(1)}, f32[512,128]{1,0:T(8,128)S(1)}, u32[]{:S(2)}, u32[]{:S(2)}) collective-permute-start(f32[512,128]{1,0:T(8,128)S(1)} %bitcast.6), channel_id=1, source_target_pairs={{0,2},{1,3},{2,0},{3,1},{4,6},{5,7},{6,4},{7,5},{8,10},{9,11},{10,... | collective-permute-start | bytes 786440 | tf_op jit(solution)/shard_map/ppermute | solution.py:338
  78.1 1.6 %collective-permute-start.2 = (f32[512,128]{1,0:T(8,128)S(1)}, f32[512,128]{1,0:T(8,128)S(1)}, u32[]{:S(2)}, u32[]{:S(2)}) collective-permute-start(f32[512,128]{1,0:T(8,128)S(1)} %get-tuple-element.13), channel_id=1, source_target_pairs={{0,2},{1,3},{2,0},{3,1},{4,6},{5,7},{6,4},{7,5},{8,10},{9,11},{10,... | collective-permute-start | bytes 786440 | tf_op jit(solution)/shard_map/ppermute | solution.py:334
  106.1 1.5 %collective-permute-start.3 = (f32[512,128]{1,0:T(8,128)S(1)}, f32[512,128]{1,0:T(8,128)S(1)}, u32[]{:S(2)}, u32[]{:S(2)}) collective-permute-start(f32[512,128]{1,0:T(8,128)S(1)} %bitcast.4), channel_id=1, source_target_pairs={{0,2},{1,3},{2,0},{3,1},{4,6},{5,7},{6,4},{7,5},{8,10},{9,11},{10,... | collective-permute-start | bytes 786440 | tf_op jit(solution)/shard_map/ppermute | solution.py:338
